TPU v7x, 32 devices: a whole 2x2x4 slice. The times are simulated.
32 devices in a mesh: wide: 8 (over y, x, core), narrow: 4 (over z).
Axes of the slice: x: 2, y: 2, z: 4, core: 2. Of those that a mesh axis runs over, the one named last changes fastest.
Arguments:
- tokens: bfloat16 [8, 1024, 1024], P('wide', 'narrow'), may hold values from -6 to 6
- memory: bfloat16 [8, 1024, 1024], P('wide', 'narrow'), may hold values from -6 to 6
- dec_ids: int32 [8, 1024], P('wide'), may hold values from 0 to 3, as said below
- enc_ids: int32 [8, 1024], P('wide'), may hold values from 0 to 3, as said below
- cotangent: bfloat16 [8, 1024, 1024], P('wide', 'narrow'), may hold values from -6 to 6
- query_weight: float32 [2, 1024, 1024], P(None, ('wide', 'narrow')), may hold values from -0.1875 to 0.1875
- query_moment: float32 [2, 1024, 1024], P(None, ('wide', 'narrow')), may hold values from -256 to 256
- query_trail: float32 [2, 1024, 1024], P(None, ('wide', 'narrow')), may hold values from -0.1875 to 0.1875
- keyval_weight: float32 [2, 1024, 1024], P(None, ('wide', 'narrow')), may hold values from -0.1875 to 0.1875
- keyval_moment: float32 [2, 1024, 1024], P(None, ('wide', 'narrow')), may hold values from -256 to 256
- keyval_trail: float32 [2, 1024, 1024], P(None, ('wide', 'narrow')), may hold values from -0.1875 to 0.1875
- output_weight: float32 [2, 1024, 1024], P(None, None, ('wide', 'narrow')), may hold values from -1.5 to 1.5
- output_moment: float32 [2, 1024, 1024], P(None, None, ('wide', 'narrow')), may hold values from -256 to 256
- output_trail: float32 [2, 1024, 1024], P(None, None, ('wide', 'narrow')), may hold values from -1.5 to 1.5
- inner_weight: float32 [1024, 5632], P(('wide', 'narrow')), may hold values from -0.1875 to 0.1875
- inner_moment: float32 [1024, 5632], P(('wide', 'narrow')), may hold values from -256 to 256
- inner_trail: float32 [1024, 5632], P(('wide', 'narrow')), may hold values from -0.1875 to 0.1875
- outer_weight: float32 [2816, 1024], P(None, ('wide', 'narrow')), may hold values from -0.109375 to 0.109375
- outer_moment: float32 [2816, 1024], P(None, ('wide', 'narrow')), may hold values from -256 to 256
- outer_trail: float32 [2816, 1024], P(None, ('wide', 'narrow')), may hold values from -0.109375 to 0.109375
- norm_gains: float32 [3, 1024], P(None, ('wide', 'narrow')), may hold values from 0.1 to 1.9
- gains_moment: float32 [3, 1024], P(None, ('wide', 'narrow')), may hold values from -256 to 256
- gains_trail: float32 [3, 1024], P(None, ('wide', 'narrow')), may hold values from 0.25 to 1.75
Outputs:
- block_out: bfloat16 [8, 1024, 1024], P('wide', 'narrow')
- input_grad: float32 [8, 1024, 1024], P('wide', 'narrow')
- memory_grad: float32 [8, 1024, 1024], P('wide', 'narrow')
- new_query: float32 [2, 1024, 1024], P(None, ('wide', 'narrow'))
- new_query_moment: float32 [2, 1024, 1024], P(None, ('wide', 'narrow'))
- new_query_trail: float32 [2, 1024, 1024], P(None, ('wide', 'narrow'))
- query_copy: bfloat16 [2, 1024, 1024], P(None, ('wide', 'narrow'))
- new_keyval: float32 [2, 1024, 1024], P(None, ('wide', 'narrow'))
- new_keyval_moment: float32 [2, 1024, 1024], P(None, ('wide', 'narrow'))
- new_keyval_trail: float32 [2, 1024, 1024], P(None, ('wide', 'narrow'))
- keyval_copy: bfloat16 [2, 1024, 1024], P(None, ('wide', 'narrow'))
- new_output: float32 [2, 1024, 1024], P(None, None, ('wide', 'narrow'))
- new_output_moment: float32 [2, 1024, 1024], P(None, None, ('wide', 'narrow'))
- new_output_trail: float32 [2, 1024, 1024], P(None, None, ('wide', 'narrow'))
- output_copy: bfloat16 [2, 1024, 1024], P(None, None, ('wide', 'narrow'))
- new_inner: float32 [1024, 5632], P(('wide', 'narrow'))
- new_inner_moment: float32 [1024, 5632], P(('wide', 'narrow'))
- new_inner_trail: float32 [1024, 5632], P(('wide', 'narrow'))
- inner_copy: bfloat16 [1024, 5632], P(('wide', 'narrow'))
- new_outer: float32 [2816, 1024], P(None, ('wide', 'narrow'))
- new_outer_moment: float32 [2816, 1024], P(None, ('wide', 'narrow'))
- new_outer_trail: float32 [2816, 1024], P(None, ('wide', 'narrow'))
- outer_copy: bfloat16 [2816, 1024], P(None, ('wide', 'narrow'))
- new_gains: float32 [3, 1024], P(None, ('wide', 'narrow'))
- new_gains_moment: float32 [3, 1024], P(None, ('wide', 'narrow'))
- new_gains_trail: float32 [3, 1024], P(None, ('wide', 'narrow'))
- gains_copy: bfloat16 [3, 1024], P(None, ('wide', 'narrow'))
Inputs may be any that keep to these rules, and one draw needn't show every extreme that they name: `dec_ids`: A row's ids never fall and each of its 4 documents holds one position or more; decoder and encoder ids of a row name the same documents. `enc_ids`: A row's ids never fall and each of its 4 documents holds one position or more.
All inputs are finite; a program needn't handle non-finite values.
Results may differ from a plain program's by a relative error of at most 0.02.
The roundings to bfloat16 on the way count: a program that leaves them out, or rounds other values in their place, can miss the bound.
Values may be sent and summed in bfloat16 or wider, within the bound.
No kernel may reach another device: no remote copies, remote signals or barrier semaphores. Data moves between devices by JAX's collectives and lax.ppermute only.
A program may use at most 256 MiB of HBM per device.

v0:
```python
import math

import jax
import jax.numpy as jnp
from jax import lax
from jax.experimental import pallas as pl
from jax.experimental.pallas import tpu as pltpu
from jax.sharding import PartitionSpec as P

HDIM = 64
PAIR = 2 * HDIM
EPS = 1e-06
NEG = -1e30
RATE = 0.02
OUTPUT_RATE = 0.15
LIMIT = 16 * 2**20
BF16 = jnp.bfloat16
F32 = jnp.float32


def dot(left, right, sides):
    return lax.dot_general(
        left, right, (((sides[0],), (sides[1],)), ((), ())), preferred_element_type=F32
    )


def matmul(left, right):
    return dot(left, right, (1, 0))


def matmul_right(left, right):
    return dot(left, right, (1, 1))


def matmul_left(left, right):
    return dot(left, right, (0, 0))


def in_group(block, group):
    low = lax.broadcasted_iota(jnp.int32, block.shape, 1) < HDIM
    turned = jnp.concatenate([block[:, HDIM:], block[:, :HDIM]], axis=1)
    zero = jnp.zeros_like(block)
    if group == 0:
        return jnp.where(low, block, zero), jnp.where(low, turned, zero)
    return jnp.where(low, zero, turned), jnp.where(low, zero, block)


def allowed(kid_ref, qid_ref, bias_ref, span, order):
    keep = kid_ref[:span] == qid_ref[...]
    if order:
        count = qid_ref.shape[1]
        keys = lax.broadcasted_iota(jnp.int32, keep.shape, 0)
        queries = lax.broadcasted_iota(jnp.int32, keep.shape, 1) + pl.program_id(0) * count
        keep &= keys <= queries
    bias_ref[:span] = jnp.where(keep, 0.0, NEG).astype(F32)


def by_span(order, count, full, body):
    if not order:
        body(full)
        return
    for number in range(full // count):
        pl.when(pl.program_id(0) == number)(lambda number=number: body((number + 1) * count))


def forward_kernel(order, query_ref, key_ref, value_ref, kid_ref, qid_ref, *rest):
    out_ref, stat_ref, bias_ref = rest
    count, width = query_ref.shape

    def body(span):
        allowed(kid_ref, qid_ref, bias_ref, span, order)
        keys = key_ref[:span]
        values = value_ref[:span].T
        for group in range(width // PAIR):
            columns = slice(group * PAIR, (group + 1) * PAIR)
            rows = slice(group * HDIM, (group + 1) * HDIM)
            block = query_ref[:, columns] * jnp.asarray(HDIM**-0.5, BF16)
            parts = []
            for side, query in enumerate(in_group(block, group)):
                logits = dot(keys, query, (1, 1)) + bias_ref[:span]
                peak = jnp.max(logits, axis=0, keepdims=True)
                weights = jnp.exp(logits - peak)
                total = jnp.sum(weights, axis=0, keepdims=True)
                probs = (weights * (1.0 / total)).astype(BF16)
                parts.append(dot(values, probs, (1, 0))[rows])
                stat_ref[0, pl.ds(2 * group + side, 1), :] = peak + jnp.log(total)
            out_ref[:, columns] = jnp.concatenate(parts, axis=0).T.astype(BF16)

    by_span(order, count, key_ref.shape[0], body)


def backward_kernel(
    order, query_ref, key_ref, value_ref, kid_ref, qid_ref, grad_ref, stat_ref, *rest
):
    dquery_ref, dkeyval_ref, bias_ref, key_sum, value_sum = rest
    count, width = query_ref.shape

    @pl.when(pl.program_id(0) == 0)
    def _():
        key_sum[...] = jnp.zeros_like(key_sum)
        value_sum[...] = jnp.zeros_like(value_sum)

    def body(span):
        allowed(kid_ref, qid_ref, bias_ref, span, order)
        keys = key_ref[:span]
        values = value_ref[:span]
        keys_turned = keys.T
        dkey, dvalue = None, None
        for group in range(width // PAIR):
            columns = slice(group * PAIR, (group + 1) * PAIR)
            rows = slice(group * HDIM, (group + 1) * HDIM)
            queries = in_group(query_ref[:, columns] * jnp.asarray(HDIM**-0.5, BF16), group)
            grads = in_group(grad_ref[:, columns], group)
            parts = []
            for side in range(2):
                logits = dot(keys, queries[side], (1, 1)) + bias_ref[:span]
                probs = jnp.exp(logits - stat_ref[0, pl.ds(2 * group + side, 1), :])
                dprobs = dot(values, grads[side], (1, 1))
                dots = jnp.sum(probs * dprobs, axis=0, keepdims=True)
                dlogits = (probs * (dprobs - dots)).astype(BF16)
                parts.append(dot(keys_turned, dlogits, (1, 0))[rows])
                more_key = dot(dlogits, queries[side], (1, 0))
                more_value = dot(probs.astype(BF16), grads[side], (1, 0))
                dkey = more_key if dkey is None else dkey + more_key
                dvalue = more_value if dvalue is None else dvalue + more_value
            dquery_ref[:, columns] = (jnp.concatenate(parts, axis=0).T * HDIM**-0.5).astype(BF16)
        key_sum[:span] += dkey
        value_sum[:span] += dvalue

    by_span(order, count, key_ref.shape[0], body)

    @pl.when(pl.program_id(0) == pl.num_programs(0) - 1)
    def _():
        dkeyval_ref[:, :PAIR] = key_sum[...].astype(BF16)
        dkeyval_ref[:, PAIR:] = value_sum[...].astype(BF16)


def attention_specs(joint, count):
    span, width = joint.shape
    q_width = width - 2 * PAIR
    query = pl.BlockSpec((count, q_width), lambda i: (i, 0))
    keys = pl.BlockSpec((span, PAIR), lambda i: (0, q_width // PAIR))
    values = pl.BlockSpec((span, PAIR), lambda i: (0, q_width // PAIR + 1))
    key_ids = pl.BlockSpec((span, 1), lambda i: (0, 0))
    query_ids = pl.BlockSpec((1, count), lambda i: (0, i))
    stat = pl.BlockSpec((1, 8, count), lambda i: (i, 0, 0))
    return q_width, [query, keys, values, key_ids, query_ids], stat


def attention(joint, key_ids, query_ids, count, order):
    span = joint.shape[0]
    q_width, specs, s_spec = attention_specs(joint, count)
    return pl.pallas_call(
        lambda *refs: forward_kernel(order, *refs),
        grid=(span // count,),
        in_specs=specs,
        out_specs=[specs[0], s_spec],
        out_shape=[
            jax.ShapeDtypeStruct((span, q_width), BF16),
            jax.ShapeDtypeStruct((span // count, 8, count), F32),
        ],
        scratch_shapes=[pltpu.VMEM((span, count), F32)],
        compiler_params=pltpu.CompilerParams(vmem_limit_bytes=2 * LIMIT),
        cost_estimate=pl.CostEstimate(
            flops=4 * span * span * q_width, bytes_accessed=8 * span * q_width, transcendentals=0
        ),
    )(joint, joint, joint, key_ids, query_ids)


def attention_back(joint, grad, stat, key_ids, query_ids, count, order):
    span = joint.shape[0]
    q_width, specs, s_spec = attention_specs(joint, count)
    whole = pl.BlockSpec((span, 2 * PAIR), lambda i: (0, 0))
    return pl.pallas_call(
        lambda *refs: backward_kernel(order, *refs),
        grid=(span // count,),
        in_specs=specs + [specs[0], s_spec],
        out_specs=[specs[0], whole],
        out_shape=[
            jax.ShapeDtypeStruct((span, q_width), BF16),
            jax.ShapeDtypeStruct((span, 2 * PAIR), BF16),
        ],
        scratch_shapes=[
            pltpu.VMEM((span, count), F32),
            pltpu.VMEM((span, PAIR), F32),
            pltpu.VMEM((span, PAIR), F32),
        ],
        compiler_params=pltpu.CompilerParams(vmem_limit_bytes=2 * LIMIT),
        cost_estimate=pl.CostEstimate(
            flops=10 * span * span * q_width, bytes_accessed=16 * span * q_width, transcendentals=0
        ),
    )(joint, joint, joint, key_ids, query_ids, grad, stat)


def flip(value, bit):
    count = lax.axis_size("wide")
    return lax.ppermute(value, "wide", [(i, i ^ (1 << bit)) for i in range(count)])


def shift(value, step):
    count = lax.axis_size("narrow")
    return lax.ppermute(value, "narrow", [(i, (i + step) % count) for i in range(count)])


def sync(*values):
    return lax.optimization_barrier(values)


def place(pieces, widths):
    rows = pieces[0][0].shape[0]
    count = 1 + max(number for _, number, _ in pieces)

    def kernel(*refs):
        first = 0
        for target, cut in zip(refs[len(pieces) :], widths):
            for source, (piece, number, begin) in zip(refs, pieces):
                low, high = max(begin, first), min(begin + piece.shape[1], first + cut)
                if low < high:
                    target[number * rows : (number + 1) * rows, low - first : high - first] = source[
                        :, low - begin : high - begin
                    ]
            first += cut

    shapes = [jax.ShapeDtypeStruct((count * rows, cut), BF16) for cut in widths]
    return small_call(kernel, shapes, [piece for piece, _, _ in pieces])


def far(value):
    return pltpu.with_memory_space_constraint(value, pltpu.HBM)


def trade(value):
    return lax.all_to_all(value, "narrow", 0, 0, tiled=True)


def spread(value):
    count = lax.axis_size("narrow")
    return trade(jnp.concatenate([value] * count, axis=0))


def near_steps():
    return sorted({1, lax.axis_size("narrow") - 1})


def far_steps():
    return [s for s in range(1, lax.axis_size("narrow")) if s not in near_steps()]


def spread_steps(value, steps):
    return {step: shift(value, step) for step in steps}


def spread_join(value, came, *widths):
    count = lax.axis_size("narrow")
    pieces = [value] + [came[step] for step in sorted(came)]
    rows, width = value.shape
    widths = widths or (width,)
    firsts = [sum(widths[:number]) for number in range(len(widths))]
    spots = (lax.axis_index("narrow") - jnp.arange(count, dtype=jnp.int32)) % count
    if rows % 16:
        whole = jnp.zeros((count, rows, width), value.dtype)
        for number, piece in enumerate(pieces):
            whole = lax.dynamic_update_index_in_dim(whole, piece, spots[number], 0)
        whole = whole.reshape(count * rows, width)
        return [whole[:, first : first + wide] for first, wide in zip(firsts, widths)]

    def kernel(spot_ref, *refs):
        for number, source in enumerate(refs[:count]):
            spot = pl.multiple_of(spot_ref[number] * rows, rows)
            for target, first, wide in zip(refs[count:], firsts, widths):
                target[pl.ds(spot, rows), :] = source[:, first : first + wide]

    whole = pl.BlockSpec(memory_space=pltpu.VMEM)
    return pl.pallas_call(
        kernel,
        in_specs=[pl.BlockSpec(memory_space=pltpu.SMEM)] + [whole] * count,
        out_specs=[whole] * len(widths),
        out_shape=[jax.ShapeDtypeStruct((count * rows, wide), value.dtype) for wide in widths],
        compiler_params=pltpu.CompilerParams(vmem_limit_bytes=LIMIT),
        cost_estimate=pl.CostEstimate(flops=0, bytes_accessed=2**22, transcendentals=0),
    )(spots, *pieces)


def tight(width):
    return -(-width // PAIR) * PAIR


def cut_columns(parts):
    count = lax.axis_size("narrow")
    rows = parts[0][0].shape[0]
    shares = [wide // count for _, _, wide in parts]
    width = sum(tight(share) for share in shares)
    arrays = list({id(part): part for part, _, _ in parts}.values())
    index = [[part is array for array in arrays].index(True) for part, _, _ in parts]

    def kernel(*refs):
        target = refs[-1]
        for number in range(count):
            first = 0
            for (_, begin, _), source, share in zip(parts, index, shares):
                low = begin + number * share
                block = refs[source][:, low : low + share]
                if share % PAIR:
                    zeros = jnp.zeros((rows, tight(share) - share), BF16)
                    block = jnp.concatenate([block, zeros], axis=1)
                target[number * rows : (number + 1) * rows, first : first + tight(share)] = block
                first += tight(share)

    return small_call(kernel, [jax.ShapeDtypeStruct((count * rows, width), BF16)], arrays)[0]


def join_columns(value, share, kinds=1):
    count = lax.axis_size("narrow")
    rows = value.shape[0] // count

    def kernel(source, target):
        for kind in range(kinds):
            for number in range(count):
                place = (kind * count + number) * share
                target[:, place : place + share] = source[
                    number * rows : (number + 1) * rows,
                    kind * tight(share) : kind * tight(share) + share,
                ]

    shape = jax.ShapeDtypeStruct((rows, kinds * share * count), BF16)
    return small_call(kernel, [shape], (value,))[0]


def vmem(*arrays):
    size = sum(math.prod(shape) * jnp.dtype(kind).itemsize for shape, kind in arrays)
    return pltpu.CompilerParams(vmem_limit_bytes=min(56 * 2**20, max(LIMIT, size + LIMIT)))


def small_call(kernel, out_shape, args):
    whole = pl.BlockSpec(memory_space=pltpu.VMEM)
    return pl.pallas_call(
        kernel,
        in_specs=[whole] * len(args),
        out_specs=[whole] * len(out_shape),
        out_shape=out_shape,
        compiler_params=vmem(*[(v.shape, v.dtype) for v in (*args, *out_shape)]),
        cost_estimate=pl.CostEstimate(flops=0, bytes_accessed=2**22, transcendentals=0),
    )(*args)


def total(value):
    count = lax.axis_size("narrow")
    return jnp.sum(value.reshape((count, -1) + value.shape[1:]).astype(F32), axis=0)


def high_bits():
    return list(range(1, lax.axis_size("wide").bit_length() - 1))


def mirror_first(value):
    return {0: value} | {1 << bit: flip(value, bit) for bit in high_bits()}


def mirror_rest(known):
    bits = high_bits()
    width = known[0].shape[1]
    middle = width // (2 * PAIR) * PAIR
    came = {}
    for order, low, high in ((bits, 0, middle), (bits[::-1], middle, width)):
        have = {0: known[0][:, low:high]}
        for bit in order:
            have |= {
                mask ^ (1 << bit): known[1 << bit][:, low:high] if mask == 0 else flip(part, bit)
                for mask, part in have.items()
            }
        came |= {(mask, low): part for mask, part in have.items() if mask not in known}
    return came


def half_rest(known, turned):
    order = high_bits()[::-1] if turned else high_bits()
    have = {0: known[0]}
    for bit in order:
        have |= {
            mask ^ (1 << bit): known[1 << bit] if mask == 0 else flip(part, bit)
            for mask, part in have.items()
        }
    return {mask: part for mask, part in have.items() if mask not in known}


def half_join(*halves):
    pieces, first = [], 0
    for known, came in halves:
        pieces += [(value, mask >> 1, first) for mask, value in (known | came).items()]
        first += known[0].shape[1]
    (own,) = place(pieces, (first,))
    return own, flip(own, 0)


def mirror_join(known, came, widths):
    pieces = [(value, mask >> 1, 0) for mask, value in known.items()]
    pieces += [(value, mask >> 1, low) for (mask, low), value in came.items()]
    return place(pieces, widths)


def turned_gains(own, other, first):
    def kernel(own_ref, other_ref, out_ref):
        half = own_ref.shape[0]
        for number, source in enumerate((own_ref, other_ref)):
            out_ref[:, number * half : (number + 1) * half] = source[...].astype(F32).T[:8]

    part = pl.BlockSpec((own.shape[0], PAIR), lambda i: (0, first // PAIR))
    return pl.pallas_call(
        kernel,
        grid=(1,),
        in_specs=[part, part],
        out_specs=pl.BlockSpec((8, 2 * own.shape[0]), lambda i: (0, 0)),
        out_shape=jax.ShapeDtypeStruct((8, 2 * own.shape[0]), F32),
    )(far(own), far(other))


def column_block(width):
    return max(b for b in range(PAIR, 1537, PAIR) if width % b == 0)


class Unit:
    def __init__(self, left, right, plane, first, width):
        self.left, self.right, self.plane, self.first, self.width = left, right, plane, first, width


def by_step(starts, values, step):
    found = values[0]
    for start, value in zip(starts[1:], values[1:]):
        found = jnp.where(step >= start, value, found)
    return found


def grad_product(lanes, rows, away, came, joint, begin=0):
    units = [unit for lane in lanes for unit in lane]
    lane_of = [number for number, lane in enumerate(lanes) for _ in lane]
    tokens, features = units[0].left.shape
    count = lax.axis_size("wide")
    cut, tall = features // count, len(rows[0])
    block = min(column_block(unit.width) for unit in units)
    counts = [unit.width // block for unit in units]
    starts = [sum(counts[:number]) for number in range(len(units))]
    lane_starts = [starts[lane_of.index(number)] for number in range(len(lanes))]
    lane_counts = [sum(unit.width for unit in lane) // block for lane in lanes]
    lefts = list({id(unit.left): unit.left for unit in units}.values())
    left_of = [[left is unit.left for left in lefts].index(True) for unit in units]

    def unit_spec(number, unit):
        return pl.BlockSpec(
            (1, tokens, block),
            lambda i: (
                unit.plane,
                0,
                jnp.clip(i - starts[number], 0, counts[number] - 1) + unit.first // block,
            ),
        )

    def away_spec(place):
        return pl.BlockSpec(
            (cut, block),
            lambda i: (by_step(lane_starts, [row[place] for row in rows], i), i + begin // block),
        )

    def lane_spec(number, height, row):
        return pl.BlockSpec(
            (height, block),
            lambda i: (row, jnp.clip(i - lane_starts[number], 0, lane_counts[number] - 1)),
        )

    side = 0 if rows[0][0] < count // 2 else 1
    in_specs = [pl.BlockSpec((tokens, features // 2), lambda i: (0, side)) for _ in lefts]
    in_specs += [unit_spec(number, unit) for number, unit in enumerate(units)]
    args = lefts + [unit.right for unit in units]
    if away is not None:
        in_specs += [away_spec(place) for place in range(tall)]
        args += [away] * tall
    at = {}
    for number, pairs in enumerate(came):
        for place in range(tall):
            at[number, place] = []
            for array, row_blocks in pairs:
                at[number, place].append(len(args))
                in_specs.append(lane_spec(number, cut, row_blocks[place]))
                args.append(array)
    widths = [sum(unit.width for unit in lane) for lane in lanes]
    if joint:
        out_specs = [pl.BlockSpec((tall * cut, block), lambda i: (0, i))]
        out_shape = [pltpu.HBM((tall * cut, sum(widths)), BF16)]
    else:
        out_specs = [lane_spec(number, tall * cut, 0) for number in range(len(lanes))]
        out_shape = [pltpu.HBM((tall * cut, width), BF16) for width in widths]

    def kernel(*refs):
        outs, turned = refs[len(args) : -1], refs[-1]
        step = pl.program_id(0)
        for number, unit in enumerate(units):
            lane = lane_of[number]

            @pl.when(step == starts[number])
            def _():
                for place, row in enumerate(rows[lane]):
                    first = (row - side * (count // 2)) * cut
                    source = refs[left_of[number]][:, first : first + cut]
                    turned[place * cut : (place + 1) * cut, :] = source.T

            @pl.when((step >= starts[number]) & (step < starts[number] + counts[number]))
            def _():
                product = dot(turned[...], refs[len(lefts) + number][0], (1, 0))
                out = outs[0] if joint else outs[lane]
                for place in range(tall):
                    part = product[place * cut : (place + 1) * cut]
                    if away is not None:
                        part += refs[len(lefts) + len(units) + place][...].astype(F32)
                    for spot in at.get((lane, place), ()):
                        part += refs[spot][...].astype(F32)
                    out[place * cut : (place + 1) * cut, :] = part.astype(BF16)

    return pl.pallas_call(
        kernel,
        grid=(sum(counts),),
        in_specs=in_specs,
        out_specs=out_specs,
        out_shape=out_shape,
        scratch_shapes=[pltpu.VMEM((tall * cut, tokens), BF16)],
        compiler_params=vmem(
            *[((2, tokens, features), BF16)] * len(lefts),
            *[((2, tokens, block), BF16)] * len(units),
            *[((2, tall * cut, block), BF16)] * (2 + len(out_shape)),
            *[((2, cut, block), BF16)] * sum(len(pairs) * tall for pairs in came),
            ((tall * cut, block), F32),
        ),
        cost_estimate=pl.CostEstimate(
            flops=2 * tall * cut * sum(widths) * tokens,
            bytes_accessed=4 * tall * cut * sum(widths),
            transcendentals=0,
        ),
    )(*[far(value) for value in args])


class Sum:
    def __init__(self, *lanes):
        bits = high_bits()
        sides = 1 << len(bits)
        self.lanes = lanes
        self.orders = [bits if number % 2 else bits[::-1] for number in range(len(lanes))]
        self.came = [[] for _ in lanes]
        self.keep = []
        for order in self.orders:
            held, lists = list(range(sides)), []
            for bit in order:
                lists.append([mask for mask in held if mask << 1 >> bit & 1])
                held = [mask for mask in held if not mask << 1 >> bit & 1]
                lists.append(held)
            self.keep.append(lists)
        rows = [[sides + mask for mask in range(sides)]] * len(lanes)
        self.state = grad_product(lanes, rows, None, [[] for _ in lanes], True)

    def over_core(self):
        self.away = flip(self.state[0], 0)
        self.state = [self.away]
        return self

    def parts(self, which, level):
        last = level == len(self.orders[0])
        lanes, rows, came, starts = [], [], [], []
        for number in which:
            lists = self.keep[number]
            row = lists[2 * level - 1] if last else lists[2 * level]
            lanes.append(self.lanes[number])
            rows.append(row)
            came.append(
                [
                    (array, [lists[2 * step + 1].index(mask) for mask in row])
                    for step, array in enumerate(self.came[number])
                ]
            )
        widths = [sum(unit.width for unit in lane) for lane in self.lanes]
        return grad_product(lanes, rows, self.away, came, last, sum(widths[: which[0]]))

    def which(self, which):
        return list(which) or list(range(len(self.lanes)))

    def add_own(self, *which):
        which = self.which(which)
        self.ready = dict(zip(which, self.parts(which, 0)))
        self.state = [self.away, self.ready]
        return self

    def sync_from(self, state):
        self.state = state
        self.away = state[0]
        if len(state) > 1:
            self.ready = state[1]
        if len(state) > 2:
            self.came = state[2]

    def over_first(self, *which):
        for number in self.which(which):
            self.came[number] = [flip(self.ready[number], self.orders[number][0])]
        self.state = [self.away, self.ready, self.came]
        return self

    def over_rest(self, *which):
        which = self.which(which)
        for level in range(1, len(self.orders[0])):
            parts = self.parts(which, level)
            for number, part in zip(which, parts):
                self.came[number] = self.came[number] + [flip(part, self.orders[number][level])]
        self.state = [self.away, self.ready, self.came]
        return self

    def whole(self, *which):
        return self.parts(self.which(which), len(self.orders[0]))[0]


def hold(sums, *values):
    flat, tree = jax.tree.flatten(([one.state for one in sums], values))
    states, values = jax.tree.unflatten(tree, lax.optimization_barrier(flat))
    for one, state in zip(sums, states):
        one.sync_from(state)
    return values


def block_order():
    count = lax.axis_size("wide")
    here = lax.axis_index("wide")
    masks = [mask << 1 for mask in range(count // 2)]
    return [here ^ mask for mask in masks + [mask + 1 for mask in masks]]


def blocks_kernel(count, spot_ref, *refs):
    for source, target in zip(refs[: len(refs) // 2], refs[len(refs) // 2 :]):
        width = source.shape[1] // count
        for number in range(count):
            spot = pl.multiple_of(spot_ref[number] * width, PAIR)
            target[:, number * width : (number + 1) * width] = source[:, pl.ds(spot, width)]


def blocks(values, spots):
    count = len(spots)
    whole = pl.BlockSpec(memory_space=pltpu.VMEM)
    return pl.pallas_call(
        lambda *refs: blocks_kernel(count, *refs),
        in_specs=[pl.BlockSpec(memory_space=pltpu.SMEM)] + [whole] * len(values),
        out_specs=[whole] * len(values),
        out_shape=[jax.ShapeDtypeStruct(value.shape, value.dtype) for value in values],
        compiler_params=pltpu.CompilerParams(vmem_limit_bytes=2 * LIMIT),
        cost_estimate=pl.CostEstimate(flops=0, bytes_accessed=2**22, transcendentals=0),
    )(jnp.stack(spots).astype(jnp.int32), *values)


def to_own(*values):
    return blocks(values, block_order())


def from_own(*values):
    count = lax.axis_size("wide")
    here = lax.axis_index("wide")
    places = [((j ^ here) >> 1) + ((j ^ here) & 1) * (count // 2) for j in range(count)]
    return blocks(values, places)


def all_sum_chain(value):
    return [value] + [shift(value, step) for step in range(1, lax.axis_size("narrow"))]


def all_sum_cube(value):
    count = lax.axis_size("wide")

    def over(mask):
        return lax.ppermute(value, "wide", [(i, i ^ mask) for i in range(count)])

    return [value] + [over(mask << 1) for mask in range(1, count // 2)]


def shard_place():
    return lax.axis_index("wide") * lax.axis_size("narrow") + lax.axis_index("narrow")


def matmul_block(width, first):
    fits = [b for b in range(PAIR, 1537, PAIR) if width % b == 0 and first % b == 0]
    return max(fits)


def into(value, weight, first, width, kind):
    tokens, features = value.shape
    half = features // 2
    block = matmul_block(width, first)
    if block == width:
        block //= 2

    def kernel(value_ref, own_ref, other_ref, out_ref):
        product = dot(value_ref[:, :half], own_ref[...], (1, 0))
        product += dot(value_ref[:, half:], other_ref[...], (1, 0))
        out_ref[...] = product.astype(kind)

    part = pl.BlockSpec((half, block), lambda i: (0, i + first // block))
    return pl.pallas_call(
        kernel,
        grid=(width // block,),
        in_specs=[pl.BlockSpec(value.shape, lambda i: (0, 0)), part, part],
        out_specs=pl.BlockSpec((tokens, block), lambda i: (0, i)),
        out_shape=jax.ShapeDtypeStruct((tokens, width), kind),
        compiler_params=vmem(
            (value.shape, F32), ((4, half, block), BF16), ((4, tokens, block), F32)
        ),
        cost_estimate=pl.CostEstimate(
            flops=2 * tokens * features * width,
            bytes_accessed=2 * features * width,
            transcendentals=0,
        ),
    )(value, *[far(part) for part in weight])


def out_of(value, weight, first):
    planes, tokens, width = value.shape
    half = weight[0].shape[0]
    block = matmul_block(width, first)
    if block == width and planes == 1:
        block //= 2
    steps = width // block

    def kernel(value_ref, own_ref, other_ref, out_ref):
        own = dot(value_ref[0], own_ref[...], (1, 1))
        other = dot(value_ref[0], other_ref[...], (1, 1))

        @pl.when(pl.program_id(0) == 0)
        def _():
            out_ref[:, :half] = own
            out_ref[:, half:] = other

        @pl.when(pl.program_id(0) > 0)
        def _():
            out_ref[:, :half] += own
            out_ref[:, half:] += other

    part = pl.BlockSpec((half, block), lambda i: (0, i + first // block))
    return pl.pallas_call(
        kernel,
        grid=(planes * steps,),
        in_specs=[
            pl.BlockSpec((1, tokens, block), lambda i: (i // steps, 0, i % steps)),
            part,
            part,
        ],
        out_specs=pl.BlockSpec((tokens, 2 * half), lambda i: (0, 0)),
        out_shape=jax.ShapeDtypeStruct((tokens, 2 * half), F32),
        compiler_params=vmem(
            ((2, tokens, block), BF16), ((4, half, block), BF16), ((4, tokens, 2 * half), F32)
        ),
        cost_estimate=pl.CostEstimate(
            flops=4 * tokens * half * width * planes,
            bytes_accessed=4 * half * width * planes,
            transcendentals=0,
        ),
    )(value, *[far(part) for part in weight])


def feed_forward(value, weight, width):
    tokens, features = value.shape
    half = features // 2
    block = matmul_block(width, width)

    def kernel(value_ref, own_gate, other_gate, own_up, other_up, gate_ref, up_ref, act_ref):
        own, other = value_ref[:, :half], value_ref[:, half:]
        gate = dot(own, own_gate[...], (1, 0)) + dot(other, other_gate[...], (1, 0))
        up = dot(own, own_up[...], (1, 0)) + dot(other, other_up[...], (1, 0))
        gate_ref[...] = gate
        up_ref[...] = up
        act_ref[...] = gated(gate, up).astype(BF16)

    gate_part = pl.BlockSpec((half, block), lambda i: (0, i))
    up_part = pl.BlockSpec((half, block), lambda i: (0, i + width // block))
    out = pl.BlockSpec((tokens, block), lambda i: (0, i))
    return pl.pallas_call(
        kernel,
        grid=(width // block,),
        in_specs=[pl.BlockSpec(value.shape, lambda i: (0, 0))]
        + [gate_part, gate_part, up_part, up_part],
        out_specs=[out] * 3,
        out_shape=[jax.ShapeDtypeStruct((tokens, width), kind) for kind in (F32, F32, BF16)],
        compiler_params=vmem(((8, half, block), BF16), ((9, tokens, block), F32)),
        cost_estimate=pl.CostEstimate(
            flops=4 * tokens * features * width,
            bytes_accessed=4 * features * width,
            transcendentals=0,
        ),
    )(value, *[far(part) for part in (*weight, *weight)])


def feed_back(value, weight, gate, up):
    tokens, features = value.shape
    half = features // 2
    width = gate.shape[1]
    block = matmul_block(width, 0)

    def kernel(value_ref, own_ref, other_ref, gate_ref, up_ref, out_ref):
        grad = dot(value_ref[:, :half], own_ref[...], (1, 0))
        grad += dot(value_ref[:, half:], other_ref[...], (1, 0))
        dgate, dup = jax.vjp(gated, gate_ref[...], up_ref[...])[1](grad)
        out_ref[0] = dgate.astype(BF16)
        out_ref[1] = dup.astype(BF16)

    part = pl.BlockSpec((half, block), lambda i: (0, i))
    wide = pl.BlockSpec((tokens, block), lambda i: (0, i))
    return pl.pallas_call(
        kernel,
        grid=(width // block,),
        in_specs=[pl.BlockSpec(value.shape, lambda i: (0, 0)), part, part, wide, wide],
        out_specs=pl.BlockSpec((2, tokens, block), lambda i: (0, 0, i)),
        out_shape=jax.ShapeDtypeStruct((2, tokens, width), BF16),
        compiler_params=vmem(((4, half, block), BF16), ((9, tokens, block), F32)),
        cost_estimate=pl.CostEstimate(
            flops=2 * tokens * features * width,
            bytes_accessed=4 * features * width,
            transcendentals=0,
        ),
    )(value, *[far(part) for part in weight], gate, up)


def rms_norm(hidden, gain):
    return hidden * lax.rsqrt(jnp.mean(hidden * hidden, axis=-1, keepdims=True) + EPS) * gain


def gated(gate, up):
    return jax.nn.gelu(gate) * up


def advance(master, moment, trail, grad, rate):
    new_moment = 0.5 * moment + 0.5 * grad
    new_master = master - rate * (grad + 0.5 * new_moment)
    new_trail = 0.5 * trail + 0.5 * new_master
    return (new_master, new_moment, new_trail, new_master.astype(BF16))


def on_device(
    tokens,
    memory,
    dec_ids,
    enc_ids,
    cotangent,
    query_weight,
    query_moment,
    query_trail,
    keyval_weight,
    keyval_moment,
    keyval_trail,
    output_weight,
    output_moment,
    output_trail,
    inner_weight,
    inner_moment,
    inner_trail,
    outer_weight,
    outer_moment,
    outer_trail,
    norm_gains,
    gains_moment,
    gains_trail,
):
    rows, local_len, width = tokens.shape
    mem_local = memory.shape[1]
    narrow_count = lax.axis_size("narrow")
    seq_len = local_len * narrow_count
    inner_width = outer_weight.shape[0]
    q_width, kv_width = query_weight.shape[2], keyval_weight.shape[2]
    gain_count, gain_width = norm_gains.shape
    q_share, kv_share = q_width // narrow_count, kv_width // (2 * narrow_count)

    gain_cols = jnp.pad(norm_gains.astype(BF16).T, ((0, 0), (0, PAIR - gain_count)))
    shard0 = jnp.concatenate(
        [query_weight[0].astype(BF16), keyval_weight[0].astype(BF16), gain_cols], axis=1
    )
    z0 = spread_steps(shard0, near_steps() + far_steps())
    shard1 = jnp.concatenate(
        [
            output_weight[0].T.astype(BF16),
            query_weight[1].astype(BF16),
            keyval_weight[1].astype(BF16),
            output_weight[1].T.astype(BF16),
        ],
        axis=1,
    )
    tokens_own, memory_own, grad_ffn = to_own(
        tokens.reshape(local_len, width),
        memory.reshape(mem_local, width),
        cotangent.reshape(local_len, width),
    )
    z0, shard1, tokens_own, memory_own, grad_ffn = sync(
        z0, shard1, tokens_own, memory_own, grad_ffn
    )
    dec_col, dec_row = dec_ids.reshape(-1, 1), dec_ids.reshape(1, -1)
    enc_col = enc_ids.reshape(-1, 1)
    g0 = mirror_first(*spread_join(shard0, z0))
    z1 = spread_steps(shard1, near_steps())
    shard2 = inner_weight.astype(BF16)
    shard3 = outer_weight.T.astype(BF16)
    hidden = tokens_own.astype(F32)
    g0, z1, shard1, shard2, shard3 = sync(g0, z1, shard1, shard2, shard3)
    r0 = mirror_rest(g0)
    z1 |= spread_steps(shard1, far_steps())
    r0, z1 = sync(r0, z1)
    (own,) = mirror_join(g0, r0, (q_width + kv_width + PAIR,))
    w_zero = (own, flip(own, 0))
    a1, b1 = spread_join(shard1, z1, width + q_width, kv_width + width)
    a1 = mirror_first(a1)
    z2 = spread_steps(shard2, near_steps())
    w_zero, b1 = sync(w_zero, b1)
    gains = turned_gains(*w_zero, q_width + kv_width)
    normed_one = rms_norm(hidden, gains[0]).astype(BF16)
    half_kv = kv_width // 2
    made = into(normed_one, w_zero, 0, q_width + kv_width, BF16)
    pieces = cut_columns(
        [(made, 0, q_width), (made, q_width, half_kv), (made, q_width + half_kv, half_kv)]
    )
    pieces, a1, b1, shard2, z2 = sync(pieces, a1, b1, shard2, z2)
    joint_one = trade(pieces)
    b1 = mirror_first(b1)
    joint_one, b1, shard2 = sync(joint_one, b1, shard2)
    ra1, rb1 = half_rest(a1, False), half_rest(b1, True)
    z2 |= spread_steps(shard2, far_steps())
    context, stat_one = attention(joint_one, dec_col, dec_row, local_len, True)
    context, ra1, rb1, z2 = sync(context, ra1, rb1, z2)
    came = trade(context)
    w_one = half_join((a1, ra1), (b1, rb1))
    a2, b2 = spread_join(shard2, z2, inner_width, inner_width)
    a2 = mirror_first(a2)
    kv_at, o_two_at = width + q_width, width + q_width + kv_width
    keyval_two = into(memory_own, w_one, kv_at, kv_width, BF16)
    came, w_one, shard3, b2, keyval_two = sync(came, w_one, shard3, b2, keyval_two)
    context_one = join_columns(came, q_share)
    after_one = hidden + out_of(context_one[None], w_one, 0)
    normed_two = rms_norm(after_one, gains[1]).astype(BF16)
    query_two = into(normed_two, w_one, width, q_width, BF16)
    pieces = cut_columns(
        [(query_two, 0, q_width), (keyval_two, 0, half_kv), (keyval_two, half_kv, half_kv)]
    )
    a2, pieces, after_one, b2 = sync(a2, pieces, after_one, b2)
    joint_two = trade(pieces)
    b2 = mirror_first(b2)
    joint_two, b2, shard3 = sync(joint_two, b2, shard3)
    ra2, rb2 = half_rest(a2, False), half_rest(b2, True)
    z3 = spread_steps(shard3, near_steps() + far_steps())
    context, stat_two = attention(joint_two, enc_col, dec_row, local_len, False)
    context, ra2, rb2, z3, shard3 = sync(context, ra2, rb2, z3, shard3)
    came = trade(context)
    half_inner = inner_width // 2
    a3, b3 = spread_join(shard3, z3, half_inner, half_inner)
    a3 = mirror_first(a3)
    w_in = half_join((a2, ra2), (b2, rb2))
    came, w_in, a3, b3 = sync(came, w_in, a3, b3)
    b3 = mirror_first(b3)
    context_two = join_columns(came, q_share)
    after_two = after_one + out_of(context_two[None], w_one, o_two_at)
    normed_three = rms_norm(after_two, gains[2]).astype(BF16)
    b3, normed_three, after_two = sync(b3, normed_three, after_two)
    ra3, rb3 = half_rest(a3, False), half_rest(b3, True)
    gate, up, activated = feed_forward(normed_three, w_in, inner_width)
    ra3, rb3, gate, up, activated = sync(ra3, rb3, gate, up, activated)
    w_out = half_join((a3, ra3), (b3, rb3))
    sum_outs = Sum(
        [Unit(grad_ffn, activated[None], 0, 0, half_inner)],
        [Unit(grad_ffn, activated[None], 0, half_inner, half_inner)],
    )
    w_out, activated = hold([sum_outs], w_out, activated)
    sum_outs.over_core()
    grad_inner = feed_back(grad_ffn, w_out, gate, up)
    (grad_inner,) = hold([sum_outs], grad_inner)
    sum_outs.add_own()
    sum_ins = Sum(
        [Unit(normed_three, grad_inner, 0, 0, half_inner)],
        [Unit(normed_three, grad_inner, 0, half_inner, half_inner)],
        [Unit(normed_three, grad_inner, 1, 0, half_inner)],
        [Unit(normed_three, grad_inner, 1, half_inner, half_inner)],
    )
    (grad_inner,) = hold([sum_outs, sum_ins], grad_inner)
    sum_outs.over_first()
    sum_ins.over_core()
    grad_normed = out_of(grad_inner, w_in, 0)
    grad_hidden, grad_gain_three = jax.vjp(rms_norm, after_two, gains[2])[1](grad_normed)
    grad_two = grad_ffn.astype(F32) + grad_hidden
    grad_branch = grad_two.astype(BF16)
    pieces = cut_columns([(into(grad_branch, w_one, o_two_at, width, BF16), 0, width)])
    pieces, grad_branch_two = hold([sum_ins, sum_outs], pieces, grad_branch)
    grad_context = trade(pieces)
    sum_outs.over_rest()
    sum_ins.add_own()
    outer_whole = sum_outs.whole()
    grad_context, outer_whole = hold([sum_ins], grad_context, outer_whole)
    sum_ins.over_first(0, 1)
    outer_parts = trade(outer_whole)
    dquery, dkeyval = attention_back(
        joint_two, grad_context, stat_two, enc_col, dec_row, local_len, False
    )
    dquery, dkeyval, activated, outer_parts = hold(
        [sum_ins], dquery, dkeyval, activated, outer_parts
    )
    came = trade(dquery)
    sum_ins.over_first(2, 3)
    result = after_two + out_of(activated[None], w_out, 0)
    (block_out,) = from_own(result.astype(BF16))
    came, dkeyval, block_out = hold([sum_ins], came, dkeyval, block_out)
    came_too = trade(dkeyval)
    sum_ins.over_rest()
    query_grad_two = join_columns(came, q_share)
    grad_normed_two = out_of(query_grad_two[None], w_one, width)
    grad_hidden, grad_gain_two = jax.vjp(rms_norm, after_one, gains[1])[1](grad_normed_two)
    grad_one = grad_two + grad_hidden
    grad_branch = grad_one.astype(BF16)
    pieces = cut_columns([(into(grad_branch, w_one, 0, width, BF16), 0, width)])
    pieces, grad_branch, came_too = hold([sum_ins], pieces, grad_branch, came_too)
    grad_context = trade(pieces)
    gate_whole = sum_ins.whole(0, 1)
    keyval_grad_two = join_columns(came_too, kv_share, 2)
    sum_mid = Sum(
        [
            Unit(grad_branch_two, context_two[None], 0, 0, width),
            Unit(memory_own, keyval_grad_two[None], 0, 0, kv_width),
        ],
        [
            Unit(normed_two, query_grad_two[None], 0, 0, q_width),
            Unit(grad_branch, context_one[None], 0, 0, width),
        ],
    )
    grad_context, keyval_grad_two, gate_whole = hold(
        [sum_mid, sum_ins], grad_context, keyval_grad_two, gate_whole
    )
    sum_mid.over_core()
    gate_parts = trade(gate_whole)
    dquery, dkeyval = attention_back(
        joint_one, grad_context, stat_one, dec_col, dec_row, local_len, True
    )
    sum_mid.add_own()
    dquery, dkeyval, keyval_grad_two, outer_parts, gate_parts = hold(
        [sum_mid], dquery, dkeyval, keyval_grad_two, outer_parts, gate_parts
    )
    came = trade(dquery)
    sum_mid.over_first()
    (memory_grad,) = from_own(out_of(keyval_grad_two[None], w_one, kv_at))
    sum_outer = total(outer_parts).T
    up_whole = sum_ins.whole(2, 3)
    came, sum_outer, memory_grad, dkeyval, up_whole = hold(
        [sum_mid], came, sum_outer, memory_grad, dkeyval, up_whole
    )
    came_too = trade(dkeyval)
    sum_mid.over_rest()
    query_grad_one = join_columns(came, q_share)
    grad_normed_one = out_of(query_grad_one[None], w_zero, 0)
    came_too, grad_normed_one = hold([sum_mid], came_too, grad_normed_one)
    keyval_grad_one = join_columns(came_too, kv_share, 2)
    sum_last = Sum(
        [Unit(normed_one, query_grad_one[None], 0, 0, q_width)],
        [Unit(normed_one, keyval_grad_one[None], 0, 0, kv_width)],
    )
    up_parts = trade(up_whole)
    mid_whole = sum_mid.whole()
    keyval_grad_one, mid_whole = hold([sum_last], keyval_grad_one, mid_whole)
    sum_last.over_core()
    mid_parts = trade(mid_whole)
    (keyval_grad_one,) = hold([sum_last], keyval_grad_one)
    sum_last.add_own()
    (keyval_grad_one,) = hold([sum_last], keyval_grad_one)
    sum_last.over_first()
    grad_normed_one += out_of(keyval_grad_one[None], w_zero, q_width)
    grad_hidden, grad_gain_one = jax.vjp(rms_norm, hidden, gains[0])[1](grad_normed_one)
    input_grad, full_gains = from_own(
        grad_one + grad_hidden,
    ) + from_own(jnp.stack([grad_gain_one, grad_gain_two, grad_gain_three]))
    input_grad, full_gains = hold([sum_last], input_grad, full_gains)
    sum_last.over_rest()
    gain_parts = all_sum_cube(full_gains)
    sum_inner = jnp.concatenate([total(gate_parts), total(up_parts)], axis=1)
    gain_parts, mid_parts = hold([sum_last], gain_parts, mid_parts)
    sum_two = total(mid_parts)
    last_parts = trade(sum_last.whole())
    part = sum(gain_parts)
    full_gains = sum(all_sum_chain(part + flip(part, 0)))
    sum_gains = lax.dynamic_slice_in_dim(full_gains, shard_place() * gain_width, gain_width, 1)
    sum_one = total(last_parts)
    after_kv, after_q = width + kv_width, width + kv_width + q_width
    sum_query = jnp.stack([sum_one[:, :q_width], sum_two[:, after_kv:after_q]])
    sum_keyval = jnp.stack([sum_one[:, q_width:], sum_two[:, width:after_kv]])
    sum_output = jnp.stack([sum_two[:, after_q:], sum_two[:, :width]]).transpose(0, 2, 1)
    block_out = block_out.reshape(rows, local_len, width)
    input_grad = input_grad.reshape(rows, local_len, width)
    memory_grad = memory_grad.reshape(rows, mem_local, width)
    token_total = rows * lax.axis_size("wide") * seq_len
    rate = RATE / math.sqrt(token_total)
    output_rate = OUTPUT_RATE / math.sqrt(token_total)
    new_query = advance(query_weight, query_moment, query_trail, sum_query, rate)
    new_keyval = advance(keyval_weight, keyval_moment, keyval_trail, sum_keyval, rate)
    new_output = advance(output_weight, output_moment, output_trail, sum_output, output_rate)
    new_inner = advance(inner_weight, inner_moment, inner_trail, sum_inner, rate)
    new_outer = advance(outer_weight, outer_moment, outer_trail, sum_outer, rate)
    new_gains = advance(norm_gains, gains_moment, gains_trail, sum_gains, rate)
    return (
        block_out,
        input_grad,
        memory_grad,
        new_query[0],
        new_query[1],
        new_query[2],
        new_query[3],
        new_keyval[0],
        new_keyval[1],
        new_keyval[2],
        new_keyval[3],
        new_output[0],
        new_output[1],
        new_output[2],
        new_output[3],
        new_inner[0],
        new_inner[1],
        new_inner[2],
        new_inner[3],
        new_outer[0],
        new_outer[1],
        new_outer[2],
        new_outer[3],
        new_gains[0],
        new_gains[1],
        new_gains[2],
        new_gains[3],
    )


def solution(mesh):
    in_specs = (
        P("wide", "narrow", None),
        P("wide", "narrow", None),
        P("wide", None),
        P("wide", None),
        P("wide", "narrow", None),
        P(None, ("wide", "narrow"), None),
        P(None, ("wide", "narrow"), None),
        P(None, ("wide", "narrow"), None),
        P(None, ("wide", "narrow"), None),
        P(None, ("wide", "narrow"), None),
        P(None, ("wide", "narrow"), None),
        P(None, None, ("wide", "narrow")),
        P(None, None, ("wide", "narrow")),
        P(None, None, ("wide", "narrow")),
        P(("wide", "narrow"), None),
        P(("wide", "narrow"), None),
        P(("wide", "narrow"), None),
        P(None, ("wide", "narrow")),
        P(None, ("wide", "narrow")),
        P(None, ("wide", "narrow")),
        P(None, ("wide", "narrow")),
        P(None, ("wide", "narrow")),
        P(None, ("wide", "narrow")),
    )
    out_specs = (
        P("wide", "narrow", None),
        P("wide", "narrow", None),
        P("wide", "narrow", None),
        P(None, ("wide", "narrow"), None),
        P(None, ("wide", "narrow"), None),
        P(None, ("wide", "narrow"), None),
        P(None, ("wide", "narrow"), None),
        P(None, ("wide", "narrow"), None),
        P(None, ("wide", "narrow"), None),
        P(None, ("wide", "narrow"), None),
        P(None, ("wide", "narrow"), None),
        P(None, None, ("wide", "narrow")),
        P(None, None, ("wide", "narrow")),
        P(None, None, ("wide", "narrow")),
        P(None, None, ("wide", "narrow")),
        P(("wide", "narrow"), None),
        P(("wide", "narrow"), None),
        P(("wide", "narrow"), None),
        P(("wide", "narrow"), None),
        P(None, ("wide", "narrow")),
        P(None, ("wide", "narrow")),
        P(None, ("wide", "narrow")),
        P(None, ("wide", "narrow")),
        P(None, ("wide", "narrow")),
        P(None, ("wide", "narrow")),
        P(None, ("wide", "narrow")),
        P(None, ("wide", "narrow")),
    )
    return jax.shard_map(
        on_device, mesh=mesh, in_specs=in_specs, out_specs=out_specs, check_vma=False
    )
```

profile of v0, /device:TPU:0, one launch (start us, length us, event | category | flops | bytes accessed | tf_op | source)
XLA Modules:
  0.0 559.0 jit_solution(2349061007920455519)
XLA Ops:
  3.6 5.1 collective-permute-start.2
  12.8 7.7 %collective-permute-done.1.refs_2_ = bf16[32,2176]{1,0:T(8,128)(2,1)S(1)} collective-permute-done((bf16[32,2176]{1,0:T(8,128)(2,1)S(1)}, bf16[32,2176]{1,0:T(8,128)(2,1)S(1)}, u32[]{:S(2)}, u32[]{:S(2)}) %collective-permute-start.1) | collective-permute-done | bytes 139296 | tf_op jit(solution)/shard_map/ppermute | solution.py:202
  28.8 6.9 %collective-permute-done.5.refs_1_ = bf16[32,4096]{1,0:T(8,128)(2,1)S(1)} collective-permute-done((bf16[32,4096]{1,0:T(8,128)(2,1)S(1)}, bf16[32,4096]{1,0:T(8,128)(2,1)S(1)}, u32[]{:S(2)}, u32[]{:S(2)}) %collective-permute-start.5) | collective-permute-done | bytes 262176 | tf_op jit(solution)/shard_map/ppermute | solution.py:202
  45.8 6.0 %collective-permute-done.9.refs_2_ = bf16[32,4096]{1,0:T(8,128)(2,1)S(1)} collective-permute-done((bf16[32,4096]{1,0:T(8,128)(2,1)S(1)}, bf16[32,4096]{1,0:T(8,128)(2,1)S(1)}, u32[]{:S(2)}, u32[]{:S(2)}) %collective-permute-start.9) | collective-permute-done | bytes 262176 | tf_op jit(solution)/shard_map/ppermute | solution.py:202
  79.0 12.3 %collective-permute-done.16.refs_6_ = bf16[128,2048]{1,0:T(8,128)(2,1)S(1)} collective-permute-done((bf16[128,2048]{1,0:T(8,128)(2,1)S(1)}, bf16[128,2048]{1,0:T(8,128)(2,1)S(1)}, u32[]{:S(2)}, u32[]{:S(2)}) %collective-permute-start.16) | collective-permute-done | bytes 524320 | tf_op jit(solution)/shard_map/ppermute | solution.py:197
  92.1 8.9 %all-to-all-done = bf16[4,256,512]{2,1,0:T(8,128)(2,1)S(1)} async-done(((bf16[4,256,512]{2,1,0:T(8,128)(2,1)}), bf16[4,256,512]{2,1,0:T(8,128)(2,1)S(1)}, u32[]{:S(2)}, u32[]{:S(2)}) %all-to-all-start) | async-done | bytes 1048608 | tf_op jit(solution)/shard_map/all_to_all | solution.py:233
  103.6 10.2 %shard_map.437 = (bf16[1024,256]{1,0:T(8,128)(2,1)S(1)}, f32[4,8,256]{2,1,0:T(8,128)S(1)}) custom-call(bf16[1024,512]{1,0:T(8,128)(2,1)S(1)} %bitcast.161, bf16[1024,512]{1,0:T(8,128)(2,1)S(1)} %bitcast.162, bf16[1024,512]{1,0:T(8,128)(2,1)S(1)} %bitcast.163, s32[1024,1]{1,0:T(8,128)S(1)} %copy-done.40, s32[1,1024]{1,0:T(1,128)S(1)} %copy-done.53), custom_call_target="tpu_custom_call" | custom-call | flops 1073741824 | bytes 2097152 | tf_op jit(solution)/shard_map/pallas_call | solution.py:153
  133.0 7.2 %all-to-all-done.1 = bf16[4,256,256]{2,1,0:T(8,128)(2,1)S(1)} async-done(((bf16[4,256,256]{2,1,0:T(8,128)(2,1)}), bf16[4,256,256]{2,1,0:T(8,128)(2,1)S(1)}, u32[]{:S(2)}, u32[]{:S(2)}) %all-to-all-start.1) | async-done | bytes 524320 | tf_op jit(solution)/shard_map/all_to_all | solution.py:233
  155.9 15.6 %collective-permute-done.24.refs_6_ = bf16[128,2816]{1,0:T(8,128)(2,1)S(1)} collective-permute-done((bf16[128,2816]{1,0:T(8,128)(2,1)S(1)}, bf16[128,2816]{1,0:T(8,128)(2,1)S(1)}, u32[]{:S(2)}, u32[]{:S(2)}) %collective-permute-start.24) | collective-permute-done | bytes 720928 | tf_op jit(solution)/shard_map/ppermute | solution.py:197
  183.1 14.1 %shard_map.445 = (bf16[1024,256]{1,0:T(8,128)(2,1)S(1)}, f32[4,8,256]{2,1,0:T(8,128)S(1)}) custom-call(bf16[1024,512]{1,0:T(8,128)(2,1)S(1)} %bitcast.167, bf16[1024,512]{1,0:T(8,128)(2,1)S(1)} %bitcast.168, bf16[1024,512]{1,0:T(8,128)(2,1)S(1)} %bitcast.169, s32[1024,1]{1,0:T(8,128)S(1)} %copy-done.42, s32[1,1024]{1,0:T(1,128)S(1)} %copy-done.53), custom_call_target="tpu_custom_call" | custom-call | flops 1073741824 | bytes 2097152 | tf_op jit(solution)/shard_map/pallas_call | solution.py:153
  210.7 9.1 %collective-permute-done.32.refs_2_ = bf16[128,1408]{1,0:T(8,128)(2,1)S(1)} collective-permute-done((bf16[128,1408]{1,0:T(8,128)(2,1)S(1)}, bf16[128,1408]{1,0:T(8,128)(2,1)S(1)}, u32[]{:S(2)}, u32[]{:S(2)}) %collective-permute-start.32) | collective-permute-done | bytes 360480 | tf_op jit(solution)/shard_map/ppermute | solution.py:197
  228.6 5.2 collective-permute-done.35.refs_6_
  234.3 6.9 %shard_map.450 = (f32[256,2816]{1,0:T(8,128)S(1)}, f32[256,2816]{1,0:T(8,128)S(1)}, bf16[256,2816]{1,0:T(8,128)(2,1)S(1)}) custom-call(bf16[256,1024]{1,0:T(8,128)(2,1)S(1)} %multiply_convert_fusion.value_ref.refs_0_, bf16[512,5632]{1,0:T(8,128)(2,1)} %shard_map.446.own_gate.own_up.own_ref, ...), custom_call_target="tpu_custom_call" | custom-call | flops 2952790016 | bytes 11534336 | tf_op jit(solution)/shard_map/pallas_call | solution.py:774
  242.3 5.1 shard_map.451
  249.2 5.6 %shard_map.453.refs_1_.refs_2_.refs_3_.refs_4_.value_ref = bf16[2,256,2816]{2,1,0:T(8,128)(2,1)S(1)} custom-call(bf16[256,1024]{1,0:T(8,128)(2,1)S(1)} %copy-done.8, bf16[512,2816]{1,0:T(8,128)(2,1)} %copy-done.5, bf16[512,2816]{1,0:T(8,128)(2,1)} %copy-done.66, f32[256,2816]{1,0:T(8,128)S(1)} %get-tuple-element.356.gate_ref, ...), custom_call_target="tpu_custom_call" | custom-call | flops 1476395008 | bytes 11534336 | tf_op jit(solution)/shard_map/pallas_call | solution.py:805
  260.4 6.5 %shard_map.455 = bf16[512,5632]{1,0:T(8,128)(2,1)} custom-call(bf16[256,1024]{1,0:T(8,128)(2,1)} %copy-done.6, bf16[2,256,2816]{2,1,0:T(8,128)(2,1)} %copy-done, bf16[2,256,2816]{2,1,0:T(8,128)(2,1)} %copy-done, bf16[2,256,2816]{2,1,0:T(8,128)(2,1)} %copy-done, bf16[2,256,2816]{2,1,0:T(8,128)(2,1)} %copy-done), custom_call_target="tpu_custom_call" | custom-call | flops 1476395008 | bytes 11534336 | tf_op jit(solution)/shard_map/pallas_call | solution.py:517
  271.5 7.3 %shard_map.456 = f32[256,1024]{1,0:T(8,128)S(1)} custom-call(bf16[2,256,2816]{2,1,0:T(8,128)(2,1)S(1)} %copy-done.1, bf16[512,5632]{1,0:T(8,128)(2,1)} %shard_map.446.own_gate.own_up.own_ref, bf16[512,5632]{1,0:T(8,128)(2,1)} %collective-permute-done.30.other_gate.other_up.other_ref), custom_call_target="tpu_custom_call" | custom-call | flops 2952790016 | bytes 11534336 | tf_op jit(solution)/shard_map/pallas_call | solution.py:737
  295.8 6.3 %shard_map.459 = (bf16[256,1408]{1,0:T(8,128)(2,1)}, bf16[256,1408]{1,0:T(8,128)(2,1)}, bf16[256,1408]{1,0:T(8,128)(2,1)}, bf16[256,1408]{1,0:T(8,128)(2,1)}) custom-call(bf16[256,1024]{1,0:T(8,128)(2,1)} %copy-done.6, bf16[2,256,2816]{2,1,0:T(8,128)(2,1)} %copy-done, bf16[2,256,2816]{2,1,0:T(8,128)(2,1)} %copy-done, bf16[2,256,2816]{2,1,0:T(8,128)(2,1)} %copy-done, ...), custom_call_target="tpu_custom_call" | custom-call | flops 738197504 | bytes 5767168 | tf_op jit(solution)/shard_map/pallas_call | solution.py:517
  318.5 17.0 %shard_map.462 = (bf16[1024,256]{1,0:T(8,128)(2,1)S(1)}, bf16[1024,256]{1,0:T(8,128)(2,1)}) custom-call(bf16[1024,512]{1,0:T(8,128)(2,1)S(1)} %bitcast.170, bf16[1024,512]{1,0:T(8,128)(2,1)S(1)} %bitcast.171, bf16[1024,512]{1,0:T(8,128)(2,1)S(1)} %bitcast.172, s32[1024,1]{1,0:T(8,128)S(1)} %copy-done.43, s32[1,1024]{1,0:T(1,128)S(1)} %copy-done.53, ...), custom_call_target="tpu_custom_call" | custom-call | flops 2684354560 | bytes 4194304 | tf_op jit(solution)/shard_map/pallas_call | solution.py:174
  337.2 5.1 all-to-all-start.6
  350.7 6.5 %collective-permute-done.46.refs_8_.refs_4_ = bf16[256,1408]{1,0:T(8,128)(2,1)} collective-permute-done((bf16[256,1408]{1,0:T(8,128)(2,1)}, bf16[256,1408]{1,0:T(8,128)(2,1)}, u32[]{:S(2)}, u32[]{:S(2)}) %collective-permute-start.46) | collective-permute-done | bytes 720928 | tf_op jit(solution)/shard_map/ppermute | solution.py:197
  366.4 5.9 %shard_map.465 = (bf16[128,1408]{1,0:T(8,128)(2,1)}, bf16[128,1408]{1,0:T(8,128)(2,1)}, bf16[128,1408]{1,0:T(8,128)(2,1)}, bf16[128,1408]{1,0:T(8,128)(2,1)}) custom-call(bf16[256,1024]{1,0:T(8,128)(2,1)} %copy-done.6, bf16[2,256,2816]{2,1,0:T(8,128)(2,1)} %copy-done, bf16[2,256,2816]{2,1,0:T(8,128)(2,1)} %copy-done, bf16[2,256,2816]{2,1,0:T(8,128)(2,1)} %copy-done, ...), custom_call_target="tpu_custom_call" | custom-call | flops 369098752 | bytes 2883584 | tf_op jit(solution)/shard_map/pallas_call | solution.py:517
  385.6 4.8 all-to-all-start.8
  395.0 5.8 %shard_map.471 = bf16[512,4096]{1,0:T(8,128)(2,1)} custom-call(bf16[256,1024]{1,0:T(8,128)(2,1)} %copy-done.17, bf16[256,1024]{1,0:T(8,128)(2,1)} %copy-done.23, bf16[256,1024]{1,0:T(8,128)(2,1)} %copy-done.16, bf16[256,1024]{1,0:T(8,128)(2,1)} %copy-done.18, bf16[1,256,1024]{2,1,0:T(8,128)(2,1)} %bitcast.132, bf16[1,256,1024]{2,1,0:T(8,128)(2,1)} %bitcast.141, ...), custom_call_target="tpu_custom_call" | custom-call | flops 1073741824 | bytes 8388608 | tf_op jit(solution)/shard_map/pallas_call | solution.py:517
  400.9 5.5 all-to-all-start.9
  406.4 12.2 %shard_map.474 = (bf16[1024,256]{1,0:T(8,128)(2,1)}, bf16[1024,256]{1,0:T(8,128)(2,1)}) custom-call(bf16[1024,512]{1,0:T(8,128)(2,1)S(1)} %bitcast.164, bf16[1024,512]{1,0:T(8,128)(2,1)S(1)} %bitcast.165, bf16[1024,512]{1,0:T(8,128)(2,1)S(1)} %bitcast.166, s32[1024,1]{1,0:T(8,128)S(1)} %copy-done.41, s32[1,1024]{1,0:T(1,128)S(1)} %copy-done.53, ...), custom_call_target="tpu_custom_call" | custom-call | flops 2684354560 | bytes 4194304 | tf_op jit(solution)/shard_map/pallas_call | solution.py:174
  418.7 5.8 %shard_map.473 = (bf16[256,2048]{1,0:T(8,128)(2,1)}, bf16[256,2048]{1,0:T(8,128)(2,1)}) custom-call(bf16[256,1024]{1,0:T(8,128)(2,1)} %copy-done.17, bf16[256,1024]{1,0:T(8,128)(2,1)} %copy-done.23, bf16[256,1024]{1,0:T(8,128)(2,1)} %copy-done.16, bf16[256,1024]{1,0:T(8,128)(2,1)} %copy-done.18, bf16[1,256,1024]{2,1,0:T(8,128)(2,1)} %bitcast.133, ...), custom_call_target="tpu_custom_call" | custom-call | flops 536870912 | bytes 4194304 | tf_op jit(solution)/shard_map/pallas_call | solution.py:517
  441.3 5.1 all-to-all-done.10
  457.8 5.4 shard_map.479
  478.7 5.7 %shard_map.483 = bf16[128,4096]{1,0:T(8,128)(2,1)} custom-call(bf16[256,1024]{1,0:T(8,128)(2,1)} %copy-done.17, bf16[256,1024]{1,0:T(8,128)(2,1)} %copy-done.23, bf16[256,1024]{1,0:T(8,128)(2,1)} %copy-done.16, bf16[256,1024]{1,0:T(8,128)(2,1)} %copy-done.18, bf16[1,256,1024]{2,1,0:T(8,128)(2,1)} %bitcast.135, bf16[1,256,1024]{2,1,0:T(8,128)(2,1)} %bitcast.144, ...), custom_call_target="tpu_custom_call" | custom-call | flops 268435456 | bytes 2097152 | tf_op jit(solution)/shard_map/pallas_call | solution.py:517
  510.2 7.1 %collective-permute-done.58.refs_4_ = bf16[256,1024]{1,0:T(8,128)(2,1)S(1)} collective-permute-done((bf16[256,1024]{1,0:T(8,128)(2,1)S(1)}, bf16[256,1024]{1,0:T(8,128)(2,1)S(1)}, u32[]{:S(2)}, u32[]{:S(2)}) %collective-permute-start.58) | collective-permute-done | bytes 524320 | tf_op jit(solution)/shard_map/ppermute | solution.py:197
  536.8 4.9 all-to-all-start.13
  (502 shorter events, 313.8 us)
Async XLA Ops:
  52.2 18.9 %collective-permute-start.14 = (bf16[32,5632]{1,0:T(8,128)(2,1)}, bf16[32,5632]{1,0:T(8,128)(2,1)}, u32[]{:S(2)}, u32[]{:S(2)}) collective-permute-start(bf16[32,5632]{1,0:T(8,128)(2,1)} %convert_element_type.120.refs_0_), channel_id=1, source_target_pairs={{0,3},{1,0},{2,1},{3,2},{4,7},{5,4},{6,5},{7,6},{8,11},{9,8},{10,9... | collective-permute-start | bytes 1081352 | tf_op jit(solution)/shard_map/ppermute | solution.py:202
  71.8 29.2 %all-to-all-start = ((bf16[4,256,512]{2,1,0:T(8,128)(2,1)}), bf16[4,256,512]{2,1,0:T(8,128)(2,1)S(1)}, u32[]{:S(2)}, u32[]{:S(2)}) async-start(bf16[4,256,512]{2,1,0:T(8,128)(2,1)} %bitcast.22), calls=%async_computation | async-start | bytes 2097152 | tf_op jit(solution)/shard_map/all_to_all | solution.py:233
  77.7 36.1 %collective-permute-start.17 = (bf16[128,2048]{1,0:T(8,128)(2,1)}, bf16[128,2048]{1,0:T(8,128)(2,1)}, u32[]{:S(2)}, u32[]{:S(2)}) collective-permute-start(bf16[128,2048]{1,0:T(8,128)(2,1)} %collective-permute-done.11.refs_1_), channel_id=1, source_target_pairs={{0,16},{4,20},{8,24},{12,28},{16,0},{20,4},{24,8},{28,12},{1,17},{... | collective-permute-start | bytes 1572872 | tf_op jit(solution)/shard_map/ppermute | solution.py:197
  121.1 19.1 %all-to-all-start.1 = ((bf16[4,256,256]{2,1,0:T(8,128)(2,1)}), bf16[4,256,256]{2,1,0:T(8,128)(2,1)S(1)}, u32[]{:S(2)}, u32[]{:S(2)}) async-start(bf16[4,256,256]{2,1,0:T(8,128)(2,1)} %bitcast.179), calls=%async_computation.1 | async-start | bytes 1048576 | tf_op jit(solution)/shard_map/all_to_all | solution.py:233
  128.1 19.5 %collective-permute-start.21 = (bf16[128,2816]{1,0:T(8,128)(2,1)}, bf16[128,2816]{1,0:T(8,128)(2,1)S(1)}, u32[]{:S(2)}, u32[]{:S(2)}) collective-permute-start(bf16[128,2816]{1,0:T(8,128)(2,1)} %get-tuple-element.323.refs_0_), channel_id=1, source_target_pairs={{0,16},{4,20},{8,24},{12,28},{16,0},{20,4},{24,8},{28,12},{1,17},{... | collective-permute-start | bytes 2162696 | tf_op jit(solution)/shard_map/ppermute | solution.py:197
  129.3 18.3 %collective-permute-start.20 = (bf16[128,2816]{1,0:T(8,128)(2,1)}, bf16[128,2816]{1,0:T(8,128)(2,1)}, u32[]{:S(2)}, u32[]{:S(2)}) collective-permute-start(bf16[128,2816]{1,0:T(8,128)(2,1)} %get-tuple-element.323.refs_0_), channel_id=1, source_target_pairs={{0,8},{4,12},{8,0},{12,4},{16,24},{20,28},{24,16},{28,20},{1,9},{5... | collective-permute-start | bytes 2162696 | tf_op jit(solution)/shard_map/ppermute | solution.py:197
  147.6 29.4 %all-to-all-start.2 = ((bf16[4,256,512]{2,1,0:T(8,128)(2,1)}), bf16[4,256,512]{2,1,0:T(8,128)(2,1)S(1)}, u32[]{:S(2)}, u32[]{:S(2)}) async-start(bf16[4,256,512]{2,1,0:T(8,128)(2,1)} %bitcast.29), calls=%async_computation.2 | async-start | bytes 2097152 | tf_op jit(solution)/shard_map/all_to_all | solution.py:233
  152.4 19.1 %collective-permute-start.24 = (bf16[128,2816]{1,0:T(8,128)(2,1)S(1)}, bf16[128,2816]{1,0:T(8,128)(2,1)S(1)}, u32[]{:S(2)}, u32[]{:S(2)}) collective-permute-start(bf16[128,2816]{1,0:T(8,128)(2,1)S(1)} %get-tuple-element.326.refs_4_), channel_id=1, source_target_pairs={{0,16},{4,20},{8,24},{12,28},{16,0},{20,4},{24,8},{28,12},{1,17},{... | collective-permute-start | bytes 2162696 | tf_op jit(solution)/shard_map/ppermute | solution.py:197
  153.2 19.1 %collective-permute-start.23 = (bf16[128,2816]{1,0:T(8,128)(2,1)S(1)}, bf16[128,2816]{1,0:T(8,128)(2,1)S(1)}, u32[]{:S(2)}, u32[]{:S(2)}) collective-permute-start(bf16[128,2816]{1,0:T(8,128)(2,1)S(1)} %get-tuple-element.326.refs_4_), channel_id=1, source_target_pairs={{0,8},{4,12},{8,0},{12,4},{16,24},{20,28},{24,16},{28,20},{1,9},{5... | collective-permute-start | bytes 2162696 | tf_op jit(solution)/shard_map/ppermute | solution.py:197
  154.7 43.3 %collective-permute-start.25 = (bf16[128,2816]{1,0:T(8,128)(2,1)}, bf16[128,2816]{1,0:T(8,128)(2,1)}, u32[]{:S(2)}, u32[]{:S(2)}) collective-permute-start(bf16[128,2816]{1,0:T(8,128)(2,1)} %collective-permute-done.20.refs_1_), channel_id=1, source_target_pairs={{0,16},{4,20},{8,24},{12,28},{16,0},{20,4},{24,8},{28,12},{1,17},{... | collective-permute-start | bytes 2162696 | tf_op jit(solution)/shard_map/ppermute | solution.py:197
  177.0 21.0 %collective-permute-start.26 = (bf16[128,2816]{1,0:T(8,128)(2,1)}, bf16[128,2816]{1,0:T(8,128)(2,1)}, u32[]{:S(2)}, u32[]{:S(2)}) collective-permute-start(bf16[128,2816]{1,0:T(8,128)(2,1)} %copy-done.29), channel_id=1, source_target_pairs={{0,8},{4,12},{8,0},{12,4},{16,24},{20,28},{24,16},{28,20},{1,9},{5... | collective-permute-start | bytes 2162696 | tf_op jit(solution)/shard_map/ppermute | solution.py:197
  178.7 19.4 %collective-permute-start.29 = (bf16[32,2816]{1,0:T(8,128)(2,1)S(1)}, bf16[32,2816]{1,0:T(8,128)(2,1)S(1)}, u32[]{:S(2)}, u32[]{:S(2)}) collective-permute-start(bf16[32,2816]{1,0:T(8,128)(2,1)S(1)} %copy-done.28), channel_id=1, source_target_pairs={{0,3},{1,0},{2,1},{3,2},{4,7},{5,4},{6,5},{7,6},{8,11},{9,8},{10,9... | collective-permute-start | bytes 540680 | tf_op jit(solution)/shard_map/ppermute | solution.py:202
  180.0 18.0 %collective-permute-start.28 = (bf16[32,2816]{1,0:T(8,128)(2,1)S(1)}, bf16[32,2816]{1,0:T(8,128)(2,1)}, u32[]{:S(2)}, u32[]{:S(2)}) collective-permute-start(bf16[32,2816]{1,0:T(8,128)(2,1)S(1)} %copy-done.28), channel_id=1, source_target_pairs={{0,2},{1,3},{2,0},{3,1},{4,6},{5,7},{6,4},{7,5},{8,10},{9,11},{10,... | collective-permute-start | bytes 540680 | tf_op jit(solution)/shard_map/ppermute | solution.py:202
  180.0 18.0 %collective-permute-start.27 = (bf16[32,2816]{1,0:T(8,128)(2,1)S(1)}, bf16[32,2816]{1,0:T(8,128)(2,1)}, u32[]{:S(2)}, u32[]{:S(2)}) collective-permute-start(bf16[32,2816]{1,0:T(8,128)(2,1)S(1)} %copy-done.28), channel_id=1, source_target_pairs={{0,1},{1,2},{2,3},{3,0},{4,5},{5,6},{6,7},{7,4},{8,9},{9,10},{10,1... | collective-permute-start | bytes 540680 | tf_op jit(solution)/shard_map/ppermute | solution.py:202
  202.8 19.6 %collective-permute-start.30 = (bf16[512,5632]{1,0:T(8,128)(2,1)}, bf16[512,5632]{1,0:T(8,128)(2,1)}, u32[]{:S(2)}, u32[]{:S(2)}) collective-permute-start(bf16[512,5632]{1,0:T(8,128)(2,1)} %shard_map.446.own_gate.own_up.own_ref), channel_id=1, source_target_pairs={{0,4},{4,0},{8,12},{12,8},{16,20},{20,16},{24,28},{28,24},{1,5},{5... | collective-permute-start | bytes 17301512 | tf_op jit(solution)/shard_map/ppermute | solution.py:197
  202.9 19.6 %all-to-all-start.3 = ((bf16[4,256,256]{2,1,0:T(8,128)(2,1)}), bf16[4,256,256]{2,1,0:T(8,128)(2,1)S(1)}, u32[]{:S(2)}, u32[]{:S(2)}) async-start(bf16[4,256,256]{2,1,0:T(8,128)(2,1)} %bitcast.178), calls=%async_computation.3 | async-start | bytes 1048576 | tf_op jit(solution)/shard_map/all_to_all | solution.py:233
  266.9 19.4 %collective-permute-start.39 = (bf16[512,5632]{1,0:T(8,128)(2,1)}, bf16[512,5632]{1,0:T(8,128)(2,1)}, u32[]{:S(2)}, u32[]{:S(2)}) collective-permute-start(bf16[512,5632]{1,0:T(8,128)(2,1)} %shard_map.455), channel_id=1, source_target_pairs={{0,4},{4,0},{8,12},{12,8},{16,20},{20,16},{24,28},{28,24},{1,5},{5... | collective-permute-start | bytes 17301512 | tf_op jit(solution)/shard_map/ppermute | solution.py:197
  267.2 18.5 %collective-permute-start.40 = (bf16[256,1408]{1,0:T(8,128)(2,1)S(1)}, bf16[256,1408]{1,0:T(8,128)(2,1)S(1)}, u32[]{:S(2)}, u32[]{:S(2)}) collective-permute-start(bf16[256,1408]{1,0:T(8,128)(2,1)S(1)} %copy-done.118), channel_id=1, source_target_pairs={{0,16},{4,20},{8,24},{12,28},{16,0},{20,4},{24,8},{28,12},{1,17},{... | collective-permute-start | bytes 2162696 | tf_op jit(solution)/shard_map/ppermute | solution.py:197
  268.2 18.1 %collective-permute-start.41 = (bf16[256,1408]{1,0:T(8,128)(2,1)S(1)}, bf16[256,1408]{1,0:T(8,128)(2,1)S(1)}, u32[]{:S(2)}, u32[]{:S(2)}) collective-permute-start(bf16[256,1408]{1,0:T(8,128)(2,1)S(1)} %copy-done.117), channel_id=1, source_target_pairs={{0,8},{4,12},{8,0},{12,4},{16,24},{20,28},{24,16},{28,20},{1,9},{5... | collective-permute-start | bytes 2162696 | tf_op jit(solution)/shard_map/ppermute | solution.py:197
  286.3 22.2 %all-to-all-start.4 = ((bf16[4,256,256]{2,1,0:T(8,128)(2,1)}), bf16[4,256,256]{2,1,0:T(8,128)(2,1)S(1)}, u32[]{:S(2)}, u32[]{:S(2)}) async-start(bf16[4,256,256]{2,1,0:T(8,128)(2,1)} %bitcast.37), calls=%async_computation.4 | async-start | bytes 1048576 | tf_op jit(solution)/shard_map/all_to_all | solution.py:233
  308.5 28.7 %all-to-all-start.5 = ((bf16[4,32,2816]{2,1,0:T(8,128)(2,1)}), bf16[4,32,2816]{2,1,0:T(8,128)(2,1)}, u32[]{:S(2)}, u32[]{:S(2)}) async-start(bf16[4,32,2816]{2,1,0:T(8,128)(2,1)} %bitcast.183), calls=%async_computation.5 | async-start | bytes 1441792 | tf_op jit(solution)/shard_map/all_to_all | solution.py:233
  313.2 23.1 %collective-permute-start.44 = (bf16[256,1408]{1,0:T(8,128)(2,1)}, bf16[256,1408]{1,0:T(8,128)(2,1)S(1)}, u32[]{:S(2)}, u32[]{:S(2)}) collective-permute-start(bf16[256,1408]{1,0:T(8,128)(2,1)} %get-tuple-element.380), channel_id=1, source_target_pairs={{0,16},{4,20},{8,24},{12,28},{16,0},{20,4},{24,8},{28,12},{1,17},{... | collective-permute-start | bytes 2162696 | tf_op jit(solution)/shard_map/ppermute | solution.py:197
  314.4 22.7 %collective-permute-start.45 = (bf16[256,1408]{1,0:T(8,128)(2,1)}, bf16[256,1408]{1,0:T(8,128)(2,1)}, u32[]{:S(2)}, u32[]{:S(2)}) collective-permute-start(bf16[256,1408]{1,0:T(8,128)(2,1)} %get-tuple-element.381), channel_id=1, source_target_pairs={{0,8},{4,12},{8,0},{12,4},{16,24},{20,28},{24,16},{28,20},{1,9},{5... | collective-permute-start | bytes 2162696 | tf_op jit(solution)/shard_map/ppermute | solution.py:197
  337.2 20.6 %all-to-all-start.6 = ((bf16[4,256,256]{2,1,0:T(8,128)(2,1)}), bf16[4,256,256]{2,1,0:T(8,128)(2,1)}, u32[]{:S(2)}, u32[]{:S(2)}) async-start(bf16[4,256,256]{2,1,0:T(8,128)(2,1)} %bitcast.176), calls=%async_computation.6 | async-start | bytes 1048576 | tf_op jit(solution)/shard_map/all_to_all | solution.py:233
  357.8 27.8 %all-to-all-start.7 = ((bf16[4,256,256]{2,1,0:T(8,128)(2,1)}), bf16[4,256,256]{2,1,0:T(8,128)(2,1)S(1)}, u32[]{:S(2)}, u32[]{:S(2)}) async-start(bf16[4,256,256]{2,1,0:T(8,128)(2,1)} %bitcast.54), calls=%async_computation.7 | async-start | bytes 1048576 | tf_op jit(solution)/shard_map/all_to_all | solution.py:233
  400.9 25.0 %all-to-all-start.9 = ((bf16[4,32,2816]{2,1,0:T(8,128)(2,1)}), bf16[4,32,2816]{2,1,0:T(8,128)(2,1)}, u32[]{:S(2)}, u32[]{:S(2)}) async-start(bf16[4,32,2816]{2,1,0:T(8,128)(2,1)} %bitcast.182), calls=%async_computation.9 | async-start | bytes 1441792 | tf_op jit(solution)/shard_map/all_to_all | solution.py:233
  425.8 24.7 %collective-permute-start.53 = (bf16[256,2048]{1,0:T(8,128)(2,1)}, bf16[256,2048]{1,0:T(8,128)(2,1)S(1)}, u32[]{:S(2)}, u32[]{:S(2)}) collective-permute-start(bf16[256,2048]{1,0:T(8,128)(2,1)} %get-tuple-element.434), channel_id=1, source_target_pairs={{0,16},{4,20},{8,24},{12,28},{16,0},{20,4},{24,8},{28,12},{1,17},{... | collective-permute-start | bytes 3145736 | tf_op jit(solution)/shard_map/ppermute | solution.py:197
  427.0 24.5 %collective-permute-start.54 = (bf16[256,2048]{1,0:T(8,128)(2,1)}, bf16[256,2048]{1,0:T(8,128)(2,1)}, u32[]{:S(2)}, u32[]{:S(2)}) collective-permute-start(bf16[256,2048]{1,0:T(8,128)(2,1)} %get-tuple-element.435), channel_id=1, source_target_pairs={{0,8},{4,12},{8,0},{12,4},{16,24},{20,28},{24,16},{28,20},{1,9},{5... | collective-permute-start | bytes 3145736 | tf_op jit(solution)/shard_map/ppermute | solution.py:197
  451.5 18.2 %all-to-all-start.11 = ((bf16[4,256,256]{2,1,0:T(8,128)(2,1)}), bf16[4,256,256]{2,1,0:T(8,128)(2,1)S(1)}, u32[]{:S(2)}, u32[]{:S(2)}) async-start(bf16[4,256,256]{2,1,0:T(8,128)(2,1)} %bitcast.67), calls=%async_computation.11 | async-start | bytes 1048576 | tf_op jit(solution)/shard_map/all_to_all | solution.py:233
  469.7 21.7 %all-to-all-start.14 = ((bf16[4,32,2816]{2,1,0:T(8,128)(2,1)}), bf16[4,32,2816]{2,1,0:T(8,128)(2,1)S(1)}, u32[]{:S(2)}, u32[]{:S(2)}) async-start(bf16[4,32,2816]{2,1,0:T(8,128)(2,1)} %bitcast.88), calls=%async_computation.14 | async-start | bytes 1441792 | tf_op jit(solution)/shard_map/all_to_all | solution.py:233
  491.3 36.7 %all-to-all-start.12 = ((bf16[4,32,4096]{2,1,0:T(8,128)(2,1)}), bf16[4,32,4096]{2,1,0:T(8,128)(2,1)}, u32[]{:S(2)}, u32[]{:S(2)}) async-start(bf16[4,32,4096]{2,1,0:T(8,128)(2,1)} %bitcast.76), calls=%async_computation.12 | async-start | bytes 2097152 | tf_op jit(solution)/shard_map/all_to_all | solution.py:233
  536.8 18.7 %all-to-all-start.13 = ((bf16[4,32,2048]{2,1,0:T(8,128)(2,1)}), bf16[4,32,2048]{2,1,0:T(8,128)(2,1)S(1)}, u32[]{:S(2)}, u32[]{:S(2)}) async-start(bf16[4,32,2048]{2,1,0:T(8,128)(2,1)} %bitcast.184), calls=%async_computation.13 | async-start | bytes 1048576 | tf_op jit(solution)/shard_map/all_to_all | solution.py:233
  (173 other events, 1684.2 us)
where the time goes:
time: 570 us; the launch traced here: 559 us
  Pallas kernels  211 us (37%)
  waiting for transfers between devices  149 us (26%)
  starting transfers between devices  138 us (24%)
  other arithmetic  30.8 us (5%)
  local copies, waits for them, and re-layouts  28.2 us (5%)
    ppermute x51, waiting for transfers between devices, flip(): lax.ppermute(value, 'wide', [(i, i ^ 1 << bit) for i in range(count)])  82.3 us
    pallas_call x17, Pallas kernels, grad_product(): pl.pallas_call(kernel, grid=(sum(counts),), in_specs=in_specs, out_specs=...  77.9 us
    all_to_all x15, starting transfers between devices, trade(): return lax.all_to_all(value, 'narrow', 0, 0, tiled=True)  67 us
    ppermute x51, starting transfers between devices, flip(): lax.ppermute(value, 'wide', [(i, i ^ 1 << bit) for i in range(count)])  47.4 us
    all_to_all x15, waiting for transfers between devices, trade(): return lax.all_to_all(value, 'narrow', 0, 0, tiled=True)  34.7 us
    ppermute x15, waiting for transfers between devices, shift(): lax.ppermute(value, 'narrow', [(i, (i + step) % count) for i in range(cou...  31.7 us
    pallas_call x2, Pallas kernels, attention_back(): pl.pallas_call(lambda *refs: backward_kernel(order, *refs), grid=(span //...  29.3 us
    pallas_call x8, Pallas kernels, out_of(): pl.pallas_call(kernel, grid=(planes * steps,), in_specs=[pl.BlockSpec((1,...  26.5 us
  transfers between devices with their start and end apart: 84, of which 40 were waited for; matrix products, arithmetic and copies ran while one was open for 5% of the time, Pallas kernels for 34%

commit v1 on v0

--- a/solution.py
+++ b/solution.py
@@ -13,7 +13,7 @@
 NEG = -1e30
 RATE = 0.02
 OUTPUT_RATE = 0.15
-LIMIT = 16 * 2**20
+LIMIT = 10 * 2**20
 BF16 = jnp.bfloat16
 F32 = jnp.float32
 
@@ -160,7 +160,7 @@
             jax.ShapeDtypeStruct((span // count, 8, count), F32),
         ],
         scratch_shapes=[pltpu.VMEM((span, count), F32)],
-        compiler_params=pltpu.CompilerParams(vmem_limit_bytes=2 * LIMIT),
+        compiler_params=pltpu.CompilerParams(vmem_limit_bytes=24 * 2**20),
         cost_estimate=pl.CostEstimate(
             flops=4 * span * span * q_width, bytes_accessed=8 * span * q_width, transcendentals=0
         ),
@@ -185,7 +185,7 @@
             pltpu.VMEM((span, PAIR), F32),
             pltpu.VMEM((span, PAIR), F32),
         ],
-        compiler_params=pltpu.CompilerParams(vmem_limit_bytes=2 * LIMIT),
+        compiler_params=pltpu.CompilerParams(vmem_limit_bytes=24 * 2**20),
         cost_estimate=pl.CostEstimate(
             flops=10 * span * span * q_width, bytes_accessed=16 * span * q_width, transcendentals=0
         ),
@@ -276,7 +276,7 @@
         in_specs=[pl.BlockSpec(memory_space=pltpu.SMEM)] + [whole] * count,
         out_specs=[whole] * len(widths),
         out_shape=[jax.ShapeDtypeStruct((count * rows, wide), value.dtype) for wide in widths],
-        compiler_params=pltpu.CompilerParams(vmem_limit_bytes=LIMIT),
+        compiler_params=pltpu.CompilerParams(vmem_limit_bytes=16 * 2**20),
         cost_estimate=pl.CostEstimate(flops=0, bytes_accessed=2**22, transcendentals=0),
     )(spots, *pieces)
 
@@ -643,7 +643,7 @@
         in_specs=[pl.BlockSpec(memory_space=pltpu.SMEM)] + [whole] * len(values),
         out_specs=[whole] * len(values),
         out_shape=[jax.ShapeDtypeStruct(value.shape, value.dtype) for value in values],
-        compiler_params=pltpu.CompilerParams(vmem_limit_bytes=2 * LIMIT),
+        compiler_params=pltpu.CompilerParams(vmem_limit_bytes=24 * 2**20),
         cost_estimate=pl.CostEstimate(flops=0, bytes_accessed=2**22, transcendentals=0),
     )(jnp.stack(spots).astype(jnp.int32), *values)
 
@@ -868,8 +868,8 @@
 
     gain_cols = jnp.pad(norm_gains.astype(BF16).T, ((0, 0), (0, PAIR - gain_count)))
     shard0 = jnp.concatenate(
-        [query_weight[0].astype(BF16), keyval_weight[0].astype(BF16), gain_cols], axis=1
-    )
+        [query_weight[0], keyval_weight[0], gain_cols.astype(F32)], axis=1
+    ).astype(BF16)
     z0 = spread_steps(shard0, near_steps() + far_steps())
     shard1 = jnp.concatenate(
         [

time: 570 us -> 570 us (level)
  no operation moved by 1% of the time
where the time goes in v1:
time: 570 us; the launch traced here: 559 us
  Pallas kernels  211 us (37%)
  waiting for transfers between devices  149 us (26%)
  starting transfers between devices  138 us (24%)
  other arithmetic  30.9 us (5%)
  local copies, waits for them, and re-layouts  28.2 us (5%)
    ppermute x51, waiting for transfers between devices, flip(): lax.ppermute(value, 'wide', [(i, i ^ 1 << bit) for i in range(count)])  82.2 us
    pallas_call x17, Pallas kernels, grad_product(): pl.pallas_call(kernel, grid=(sum(counts),), in_specs=in_specs, out_specs=...  77.9 us
    all_to_all x15, starting transfers between devices, trade(): return lax.all_to_all(value, 'narrow', 0, 0, tiled=True)  67 us
    ppermute x51, starting transfers between devices, flip(): lax.ppermute(value, 'wide', [(i, i ^ 1 << bit) for i in range(count)])  47.4 us
    all_to_all x15, waiting for transfers between devices, trade(): return lax.all_to_all(value, 'narrow', 0, 0, tiled=True)  34.7 us
    ppermute x15, waiting for transfers between devices, shift(): lax.ppermute(value, 'narrow', [(i, (i + step) % count) for i in range(cou...  31.7 us
    pallas_call x2, Pallas kernels, attention_back(): pl.pallas_call(lambda *refs: backward_kernel(order, *refs), grid=(span //...  29.3 us
    pallas_call x8, Pallas kernels, out_of(): pl.pallas_call(kernel, grid=(planes * steps,), in_specs=[pl.BlockSpec((1,...  26.5 us
  transfers between devices with their start and end apart: 84, of which 40 were waited for; matrix products, arithmetic and copies ran while one was open for 5% of the time, Pallas kernels for 34%

profile of v1, /device:TPU:0, one launch (start us, length us, event | category | flops | bytes accessed | tf_op | source)
XLA Modules:
  0.0 559.0 jit_solution(9508826329755411221)
XLA Ops:
  3.6 5.1 collective-permute-start.2
  12.8 7.7 %collective-permute-done.1.refs_2_ = bf16[32,2176]{1,0:T(8,128)(2,1)S(1)} collective-permute-done((bf16[32,2176]{1,0:T(8,128)(2,1)S(1)}, bf16[32,2176]{1,0:T(8,128)(2,1)S(1)}, u32[]{:S(2)}, u32[]{:S(2)}) %collective-permute-start.1) | collective-permute-done | bytes 139296 | tf_op jit(solution)/shard_map/ppermute | solution.py:202
  28.8 6.9 %collective-permute-done.5.refs_1_ = bf16[32,4096]{1,0:T(8,128)(2,1)S(1)} collective-permute-done((bf16[32,4096]{1,0:T(8,128)(2,1)S(1)}, bf16[32,4096]{1,0:T(8,128)(2,1)S(1)}, u32[]{:S(2)}, u32[]{:S(2)}) %collective-permute-start.5) | collective-permute-done | bytes 262176 | tf_op jit(solution)/shard_map/ppermute | solution.py:202
  45.8 6.0 %collective-permute-done.9.refs_2_ = bf16[32,4096]{1,0:T(8,128)(2,1)S(1)} collective-permute-done((bf16[32,4096]{1,0:T(8,128)(2,1)S(1)}, bf16[32,4096]{1,0:T(8,128)(2,1)S(1)}, u32[]{:S(2)}, u32[]{:S(2)}) %collective-permute-start.9) | collective-permute-done | bytes 262176 | tf_op jit(solution)/shard_map/ppermute | solution.py:202
  79.0 12.3 %collective-permute-done.16.refs_6_ = bf16[128,2048]{1,0:T(8,128)(2,1)S(1)} collective-permute-done((bf16[128,2048]{1,0:T(8,128)(2,1)S(1)}, bf16[128,2048]{1,0:T(8,128)(2,1)S(1)}, u32[]{:S(2)}, u32[]{:S(2)}) %collective-permute-start.16) | collective-permute-done | bytes 524320 | tf_op jit(solution)/shard_map/ppermute | solution.py:197
  92.1 8.9 %all-to-all-done = bf16[4,256,512]{2,1,0:T(8,128)(2,1)S(1)} async-done(((bf16[4,256,512]{2,1,0:T(8,128)(2,1)}), bf16[4,256,512]{2,1,0:T(8,128)(2,1)S(1)}, u32[]{:S(2)}, u32[]{:S(2)}) %all-to-all-start) | async-done | bytes 1048608 | tf_op jit(solution)/shard_map/all_to_all | solution.py:233
  103.6 10.2 %shard_map.437 = (bf16[1024,256]{1,0:T(8,128)(2,1)S(1)}, f32[4,8,256]{2,1,0:T(8,128)S(1)}) custom-call(bf16[1024,512]{1,0:T(8,128)(2,1)S(1)} %bitcast.161, bf16[1024,512]{1,0:T(8,128)(2,1)S(1)} %bitcast.162, bf16[1024,512]{1,0:T(8,128)(2,1)S(1)} %bitcast.163, s32[1024,1]{1,0:T(8,128)S(1)} %copy-done.40, s32[1,1024]{1,0:T(1,128)S(1)} %copy-done.53), custom_call_target="tpu_custom_call" | custom-call | flops 1073741824 | bytes 2097152 | tf_op jit(solution)/shard_map/pallas_call | solution.py:153
  133.0 7.2 %all-to-all-done.1 = bf16[4,256,256]{2,1,0:T(8,128)(2,1)S(1)} async-done(((bf16[4,256,256]{2,1,0:T(8,128)(2,1)}), bf16[4,256,256]{2,1,0:T(8,128)(2,1)S(1)}, u32[]{:S(2)}, u32[]{:S(2)}) %all-to-all-start.1) | async-done | bytes 524320 | tf_op jit(solution)/shard_map/all_to_all | solution.py:233
  155.9 15.6 %collective-permute-done.24.refs_6_ = bf16[128,2816]{1,0:T(8,128)(2,1)S(1)} collective-permute-done((bf16[128,2816]{1,0:T(8,128)(2,1)S(1)}, bf16[128,2816]{1,0:T(8,128)(2,1)S(1)}, u32[]{:S(2)}, u32[]{:S(2)}) %collective-permute-start.24) | collective-permute-done | bytes 720928 | tf_op jit(solution)/shard_map/ppermute | solution.py:197
  183.1 14.1 %shard_map.445 = (bf16[1024,256]{1,0:T(8,128)(2,1)S(1)}, f32[4,8,256]{2,1,0:T(8,128)S(1)}) custom-call(bf16[1024,512]{1,0:T(8,128)(2,1)S(1)} %bitcast.167, bf16[1024,512]{1,0:T(8,128)(2,1)S(1)} %bitcast.168, bf16[1024,512]{1,0:T(8,128)(2,1)S(1)} %bitcast.169, s32[1024,1]{1,0:T(8,128)S(1)} %copy-done.42, s32[1,1024]{1,0:T(1,128)S(1)} %copy-done.53), custom_call_target="tpu_custom_call" | custom-call | flops 1073741824 | bytes 2097152 | tf_op jit(solution)/shard_map/pallas_call | solution.py:153
  210.7 9.1 %collective-permute-done.32.refs_2_ = bf16[128,1408]{1,0:T(8,128)(2,1)S(1)} collective-permute-done((bf16[128,1408]{1,0:T(8,128)(2,1)S(1)}, bf16[128,1408]{1,0:T(8,128)(2,1)S(1)}, u32[]{:S(2)}, u32[]{:S(2)}) %collective-permute-start.32) | collective-permute-done | bytes 360480 | tf_op jit(solution)/shard_map/ppermute | solution.py:197
  228.6 5.1 collective-permute-done.35.refs_6_
  234.3 6.9 %shard_map.450 = (f32[256,2816]{1,0:T(8,128)S(1)}, f32[256,2816]{1,0:T(8,128)S(1)}, bf16[256,2816]{1,0:T(8,128)(2,1)S(1)}) custom-call(bf16[256,1024]{1,0:T(8,128)(2,1)S(1)} %multiply_convert_fusion.value_ref.refs_0_, bf16[512,5632]{1,0:T(8,128)(2,1)} %shard_map.446.own_gate.own_up.own_ref, ...), custom_call_target="tpu_custom_call" | custom-call | flops 2952790016 | bytes 11534336 | tf_op jit(solution)/shard_map/pallas_call | solution.py:774
  242.3 5.1 shard_map.451
  249.2 5.6 %shard_map.453.refs_1_.refs_2_.refs_3_.refs_4_.value_ref = bf16[2,256,2816]{2,1,0:T(8,128)(2,1)S(1)} custom-call(bf16[256,1024]{1,0:T(8,128)(2,1)S(1)} %copy-done.8, bf16[512,2816]{1,0:T(8,128)(2,1)} %copy-done.5, bf16[512,2816]{1,0:T(8,128)(2,1)} %copy-done.66, f32[256,2816]{1,0:T(8,128)S(1)} %get-tuple-element.356.gate_ref, ...), custom_call_target="tpu_custom_call" | custom-call | flops 1476395008 | bytes 11534336 | tf_op jit(solution)/shard_map/pallas_call | solution.py:805
  260.4 6.5 %shard_map.455 = bf16[512,5632]{1,0:T(8,128)(2,1)} custom-call(bf16[256,1024]{1,0:T(8,128)(2,1)} %copy-done.6, bf16[2,256,2816]{2,1,0:T(8,128)(2,1)} %copy-done, bf16[2,256,2816]{2,1,0:T(8,128)(2,1)} %copy-done, bf16[2,256,2816]{2,1,0:T(8,128)(2,1)} %copy-done, bf16[2,256,2816]{2,1,0:T(8,128)(2,1)} %copy-done), custom_call_target="tpu_custom_call" | custom-call | flops 1476395008 | bytes 11534336 | tf_op jit(solution)/shard_map/pallas_call | solution.py:517
  271.5 7.3 %shard_map.456 = f32[256,1024]{1,0:T(8,128)S(1)} custom-call(bf16[2,256,2816]{2,1,0:T(8,128)(2,1)S(1)} %copy-done.1, bf16[512,5632]{1,0:T(8,128)(2,1)} %shard_map.446.own_gate.own_up.own_ref, bf16[512,5632]{1,0:T(8,128)(2,1)} %collective-permute-done.30.other_gate.other_up.other_ref), custom_call_target="tpu_custom_call" | custom-call | flops 2952790016 | bytes 11534336 | tf_op jit(solution)/shard_map/pallas_call | solution.py:737
  295.8 6.3 %shard_map.459 = (bf16[256,1408]{1,0:T(8,128)(2,1)}, bf16[256,1408]{1,0:T(8,128)(2,1)}, bf16[256,1408]{1,0:T(8,128)(2,1)}, bf16[256,1408]{1,0:T(8,128)(2,1)}) custom-call(bf16[256,1024]{1,0:T(8,128)(2,1)} %copy-done.6, bf16[2,256,2816]{2,1,0:T(8,128)(2,1)} %copy-done, bf16[2,256,2816]{2,1,0:T(8,128)(2,1)} %copy-done, bf16[2,256,2816]{2,1,0:T(8,128)(2,1)} %copy-done, ...), custom_call_target="tpu_custom_call" | custom-call | flops 738197504 | bytes 5767168 | tf_op jit(solution)/shard_map/pallas_call | solution.py:517
  318.5 17.0 %shard_map.462 = (bf16[1024,256]{1,0:T(8,128)(2,1)S(1)}, bf16[1024,256]{1,0:T(8,128)(2,1)}) custom-call(bf16[1024,512]{1,0:T(8,128)(2,1)S(1)} %bitcast.170, bf16[1024,512]{1,0:T(8,128)(2,1)S(1)} %bitcast.171, bf16[1024,512]{1,0:T(8,128)(2,1)S(1)} %bitcast.172, s32[1024,1]{1,0:T(8,128)S(1)} %copy-done.43, s32[1,1024]{1,0:T(1,128)S(1)} %copy-done.53, ...), custom_call_target="tpu_custom_call" | custom-call | flops 2684354560 | bytes 4194304 | tf_op jit(solution)/shard_map/pallas_call | solution.py:174
  337.2 5.1 all-to-all-start.6
  350.7 6.5 %collective-permute-done.46.refs_8_.refs_4_ = bf16[256,1408]{1,0:T(8,128)(2,1)} collective-permute-done((bf16[256,1408]{1,0:T(8,128)(2,1)}, bf16[256,1408]{1,0:T(8,128)(2,1)}, u32[]{:S(2)}, u32[]{:S(2)}) %collective-permute-start.46) | collective-permute-done | bytes 720928 | tf_op jit(solution)/shard_map/ppermute | solution.py:197
  366.4 5.9 %shard_map.465 = (bf16[128,1408]{1,0:T(8,128)(2,1)}, bf16[128,1408]{1,0:T(8,128)(2,1)}, bf16[128,1408]{1,0:T(8,128)(2,1)}, bf16[128,1408]{1,0:T(8,128)(2,1)}) custom-call(bf16[256,1024]{1,0:T(8,128)(2,1)} %copy-done.6, bf16[2,256,2816]{2,1,0:T(8,128)(2,1)} %copy-done, bf16[2,256,2816]{2,1,0:T(8,128)(2,1)} %copy-done, bf16[2,256,2816]{2,1,0:T(8,128)(2,1)} %copy-done, ...), custom_call_target="tpu_custom_call" | custom-call | flops 369098752 | bytes 2883584 | tf_op jit(solution)/shard_map/pallas_call | solution.py:517
  385.6 4.8 all-to-all-start.8
  395.0 5.8 %shard_map.471 = bf16[512,4096]{1,0:T(8,128)(2,1)} custom-call(bf16[256,1024]{1,0:T(8,128)(2,1)} %copy-done.17, bf16[256,1024]{1,0:T(8,128)(2,1)} %copy-done.23, bf16[256,1024]{1,0:T(8,128)(2,1)} %copy-done.16, bf16[256,1024]{1,0:T(8,128)(2,1)} %copy-done.18, bf16[1,256,1024]{2,1,0:T(8,128)(2,1)} %bitcast.132, bf16[1,256,1024]{2,1,0:T(8,128)(2,1)} %bitcast.141, ...), custom_call_target="tpu_custom_call" | custom-call | flops 1073741824 | bytes 8388608 | tf_op jit(solution)/shard_map/pallas_call | solution.py:517
  400.9 5.5 all-to-all-start.9
  406.4 12.2 %shard_map.474 = (bf16[1024,256]{1,0:T(8,128)(2,1)}, bf16[1024,256]{1,0:T(8,128)(2,1)}) custom-call(bf16[1024,512]{1,0:T(8,128)(2,1)S(1)} %bitcast.164, bf16[1024,512]{1,0:T(8,128)(2,1)S(1)} %bitcast.165, bf16[1024,512]{1,0:T(8,128)(2,1)S(1)} %bitcast.166, s32[1024,1]{1,0:T(8,128)S(1)} %copy-done.41, s32[1,1024]{1,0:T(1,128)S(1)} %copy-done.53, ...), custom_call_target="tpu_custom_call" | custom-call | flops 2684354560 | bytes 4194304 | tf_op jit(solution)/shard_map/pallas_call | solution.py:174
  418.7 5.8 %shard_map.473 = (bf16[256,2048]{1,0:T(8,128)(2,1)}, bf16[256,2048]{1,0:T(8,128)(2,1)}) custom-call(bf16[256,1024]{1,0:T(8,128)(2,1)} %copy-done.17, bf16[256,1024]{1,0:T(8,128)(2,1)} %copy-done.23, bf16[256,1024]{1,0:T(8,128)(2,1)} %copy-done.16, bf16[256,1024]{1,0:T(8,128)(2,1)} %copy-done.18, bf16[1,256,1024]{2,1,0:T(8,128)(2,1)} %bitcast.133, ...), custom_call_target="tpu_custom_call" | custom-call | flops 536870912 | bytes 4194304 | tf_op jit(solution)/shard_map/pallas_call | solution.py:517
  441.3 5.1 all-to-all-done.10
  457.8 5.4 shard_map.479
  478.7 5.7 %shard_map.483 = bf16[128,4096]{1,0:T(8,128)(2,1)} custom-call(bf16[256,1024]{1,0:T(8,128)(2,1)} %copy-done.17, bf16[256,1024]{1,0:T(8,128)(2,1)} %copy-done.23, bf16[256,1024]{1,0:T(8,128)(2,1)} %copy-done.16, bf16[256,1024]{1,0:T(8,128)(2,1)} %copy-done.18, bf16[1,256,1024]{2,1,0:T(8,128)(2,1)} %bitcast.135, bf16[1,256,1024]{2,1,0:T(8,128)(2,1)} %bitcast.144, ...), custom_call_target="tpu_custom_call" | custom-call | flops 268435456 | bytes 2097152 | tf_op jit(solution)/shard_map/pallas_call | solution.py:517
  510.3 7.1 %collective-permute-done.58.refs_4_ = bf16[256,1024]{1,0:T(8,128)(2,1)S(1)} collective-permute-done((bf16[256,1024]{1,0:T(8,128)(2,1)S(1)}, bf16[256,1024]{1,0:T(8,128)(2,1)S(1)}, u32[]{:S(2)}, u32[]{:S(2)}) %collective-permute-start.58) | collective-permute-done | bytes 524320 | tf_op jit(solution)/shard_map/ppermute | solution.py:197
  536.8 4.9 all-to-all-start.13
  (502 shorter events, 313.9 us)
Async XLA Ops:
  52.2 18.9 %collective-permute-start.14 = (bf16[32,5632]{1,0:T(8,128)(2,1)}, bf16[32,5632]{1,0:T(8,128)(2,1)}, u32[]{:S(2)}, u32[]{:S(2)}) collective-permute-start(bf16[32,5632]{1,0:T(8,128)(2,1)} %convert_element_type.112.refs_0_), channel_id=1, source_target_pairs={{0,3},{1,0},{2,1},{3,2},{4,7},{5,4},{6,5},{7,6},{8,11},{9,8},{10,9... | collective-permute-start | bytes 1081352 | tf_op jit(solution)/shard_map/ppermute | solution.py:202
  71.8 29.2 %all-to-all-start = ((bf16[4,256,512]{2,1,0:T(8,128)(2,1)}), bf16[4,256,512]{2,1,0:T(8,128)(2,1)S(1)}, u32[]{:S(2)}, u32[]{:S(2)}) async-start(bf16[4,256,512]{2,1,0:T(8,128)(2,1)} %bitcast.22), calls=%async_computation | async-start | bytes 2097152 | tf_op jit(solution)/shard_map/all_to_all | solution.py:233
  77.7 36.1 %collective-permute-start.17 = (bf16[128,2048]{1,0:T(8,128)(2,1)}, bf16[128,2048]{1,0:T(8,128)(2,1)}, u32[]{:S(2)}, u32[]{:S(2)}) collective-permute-start(bf16[128,2048]{1,0:T(8,128)(2,1)} %collective-permute-done.11.refs_1_), channel_id=1, source_target_pairs={{0,16},{4,20},{8,24},{12,28},{16,0},{20,4},{24,8},{28,12},{1,17},{... | collective-permute-start | bytes 1572872 | tf_op jit(solution)/shard_map/ppermute | solution.py:197
  121.1 19.1 %all-to-all-start.1 = ((bf16[4,256,256]{2,1,0:T(8,128)(2,1)}), bf16[4,256,256]{2,1,0:T(8,128)(2,1)S(1)}, u32[]{:S(2)}, u32[]{:S(2)}) async-start(bf16[4,256,256]{2,1,0:T(8,128)(2,1)} %bitcast.179), calls=%async_computation.1 | async-start | bytes 1048576 | tf_op jit(solution)/shard_map/all_to_all | solution.py:233
  128.1 19.5 %collective-permute-start.21 = (bf16[128,2816]{1,0:T(8,128)(2,1)}, bf16[128,2816]{1,0:T(8,128)(2,1)S(1)}, u32[]{:S(2)}, u32[]{:S(2)}) collective-permute-start(bf16[128,2816]{1,0:T(8,128)(2,1)} %get-tuple-element.323.refs_0_), channel_id=1, source_target_pairs={{0,16},{4,20},{8,24},{12,28},{16,0},{20,4},{24,8},{28,12},{1,17},{... | collective-permute-start | bytes 2162696 | tf_op jit(solution)/shard_map/ppermute | solution.py:197
  129.3 18.3 %collective-permute-start.20 = (bf16[128,2816]{1,0:T(8,128)(2,1)}, bf16[128,2816]{1,0:T(8,128)(2,1)}, u32[]{:S(2)}, u32[]{:S(2)}) collective-permute-start(bf16[128,2816]{1,0:T(8,128)(2,1)} %get-tuple-element.323.refs_0_), channel_id=1, source_target_pairs={{0,8},{4,12},{8,0},{12,4},{16,24},{20,28},{24,16},{28,20},{1,9},{5... | collective-permute-start | bytes 2162696 | tf_op jit(solution)/shard_map/ppermute | solution.py:197
  147.6 29.4 %all-to-all-start.2 = ((bf16[4,256,512]{2,1,0:T(8,128)(2,1)}), bf16[4,256,512]{2,1,0:T(8,128)(2,1)S(1)}, u32[]{:S(2)}, u32[]{:S(2)}) async-start(bf16[4,256,512]{2,1,0:T(8,128)(2,1)} %bitcast.29), calls=%async_computation.2 | async-start | bytes 2097152 | tf_op jit(solution)/shard_map/all_to_all | solution.py:233
  152.4 19.1 %collective-permute-start.24 = (bf16[128,2816]{1,0:T(8,128)(2,1)S(1)}, bf16[128,2816]{1,0:T(8,128)(2,1)S(1)}, u32[]{:S(2)}, u32[]{:S(2)}) collective-permute-start(bf16[128,2816]{1,0:T(8,128)(2,1)S(1)} %get-tuple-element.326.refs_4_), channel_id=1, source_target_pairs={{0,16},{4,20},{8,24},{12,28},{16,0},{20,4},{24,8},{28,12},{1,17},{... | collective-permute-start | bytes 2162696 | tf_op jit(solution)/shard_map/ppermute | solution.py:197
  153.3 19.1 %collective-permute-start.23 = (bf16[128,2816]{1,0:T(8,128)(2,1)S(1)}, bf16[128,2816]{1,0:T(8,128)(2,1)S(1)}, u32[]{:S(2)}, u32[]{:S(2)}) collective-permute-start(bf16[128,2816]{1,0:T(8,128)(2,1)S(1)} %get-tuple-element.326.refs_4_), channel_id=1, source_target_pairs={{0,8},{4,12},{8,0},{12,4},{16,24},{20,28},{24,16},{28,20},{1,9},{5... | collective-permute-start | bytes 2162696 | tf_op jit(solution)/shard_map/ppermute | solution.py:197
  154.7 43.3 %collective-permute-start.25 = (bf16[128,2816]{1,0:T(8,128)(2,1)}, bf16[128,2816]{1,0:T(8,128)(2,1)}, u32[]{:S(2)}, u32[]{:S(2)}) collective-permute-start(bf16[128,2816]{1,0:T(8,128)(2,1)} %collective-permute-done.20.refs_1_), channel_id=1, source_target_pairs={{0,16},{4,20},{8,24},{12,28},{16,0},{20,4},{24,8},{28,12},{1,17},{... | collective-permute-start | bytes 2162696 | tf_op jit(solution)/shard_map/ppermute | solution.py:197
  177.0 21.0 %collective-permute-start.26 = (bf16[128,2816]{1,0:T(8,128)(2,1)}, bf16[128,2816]{1,0:T(8,128)(2,1)}, u32[]{:S(2)}, u32[]{:S(2)}) collective-permute-start(bf16[128,2816]{1,0:T(8,128)(2,1)} %copy-done.29), channel_id=1, source_target_pairs={{0,8},{4,12},{8,0},{12,4},{16,24},{20,28},{24,16},{28,20},{1,9},{5... | collective-permute-start | bytes 2162696 | tf_op jit(solution)/shard_map/ppermute | solution.py:197
  178.7 19.4 %collective-permute-start.29 = (bf16[32,2816]{1,0:T(8,128)(2,1)S(1)}, bf16[32,2816]{1,0:T(8,128)(2,1)S(1)}, u32[]{:S(2)}, u32[]{:S(2)}) collective-permute-start(bf16[32,2816]{1,0:T(8,128)(2,1)S(1)} %copy-done.28), channel_id=1, source_target_pairs={{0,3},{1,0},{2,1},{3,2},{4,7},{5,4},{6,5},{7,6},{8,11},{9,8},{10,9... | collective-permute-start | bytes 540680 | tf_op jit(solution)/shard_map/ppermute | solution.py:202
  180.0 18.0 %collective-permute-start.28 = (bf16[32,2816]{1,0:T(8,128)(2,1)S(1)}, bf16[32,2816]{1,0:T(8,128)(2,1)}, u32[]{:S(2)}, u32[]{:S(2)}) collective-permute-start(bf16[32,2816]{1,0:T(8,128)(2,1)S(1)} %copy-done.28), channel_id=1, source_target_pairs={{0,2},{1,3},{2,0},{3,1},{4,6},{5,7},{6,4},{7,5},{8,10},{9,11},{10,... | collective-permute-start | bytes 540680 | tf_op jit(solution)/shard_map/ppermute | solution.py:202
  180.0 18.0 %collective-permute-start.27 = (bf16[32,2816]{1,0:T(8,128)(2,1)S(1)}, bf16[32,2816]{1,0:T(8,128)(2,1)}, u32[]{:S(2)}, u32[]{:S(2)}) collective-permute-start(bf16[32,2816]{1,0:T(8,128)(2,1)S(1)} %copy-done.28), channel_id=1, source_target_pairs={{0,1},{1,2},{2,3},{3,0},{4,5},{5,6},{6,7},{7,4},{8,9},{9,10},{10,1... | collective-permute-start | bytes 540680 | tf_op jit(solution)/shard_map/ppermute | solution.py:202
  202.8 19.6 %collective-permute-start.30 = (bf16[512,5632]{1,0:T(8,128)(2,1)}, bf16[512,5632]{1,0:T(8,128)(2,1)}, u32[]{:S(2)}, u32[]{:S(2)}) collective-permute-start(bf16[512,5632]{1,0:T(8,128)(2,1)} %shard_map.446.own_gate.own_up.own_ref), channel_id=1, source_target_pairs={{0,4},{4,0},{8,12},{12,8},{16,20},{20,16},{24,28},{28,24},{1,5},{5... | collective-permute-start | bytes 17301512 | tf_op jit(solution)/shard_map/ppermute | solution.py:197
  202.9 19.6 %all-to-all-start.3 = ((bf16[4,256,256]{2,1,0:T(8,128)(2,1)}), bf16[4,256,256]{2,1,0:T(8,128)(2,1)S(1)}, u32[]{:S(2)}, u32[]{:S(2)}) async-start(bf16[4,256,256]{2,1,0:T(8,128)(2,1)} %bitcast.178), calls=%async_computation.3 | async-start | bytes 1048576 | tf_op jit(solution)/shard_map/all_to_all | solution.py:233
  266.9 19.4 %collective-permute-start.39 = (bf16[512,5632]{1,0:T(8,128)(2,1)}, bf16[512,5632]{1,0:T(8,128)(2,1)}, u32[]{:S(2)}, u32[]{:S(2)}) collective-permute-start(bf16[512,5632]{1,0:T(8,128)(2,1)} %shard_map.455), channel_id=1, source_target_pairs={{0,4},{4,0},{8,12},{12,8},{16,20},{20,16},{24,28},{28,24},{1,5},{5... | collective-permute-start | bytes 17301512 | tf_op jit(solution)/shard_map/ppermute | solution.py:197
  267.2 18.5 %collective-permute-start.40 = (bf16[256,1408]{1,0:T(8,128)(2,1)S(1)}, bf16[256,1408]{1,0:T(8,128)(2,1)S(1)}, u32[]{:S(2)}, u32[]{:S(2)}) collective-permute-start(bf16[256,1408]{1,0:T(8,128)(2,1)S(1)} %copy-done.118), channel_id=1, source_target_pairs={{0,16},{4,20},{8,24},{12,28},{16,0},{20,4},{24,8},{28,12},{1,17},{... | collective-permute-start | bytes 2162696 | tf_op jit(solution)/shard_map/ppermute | solution.py:197
  268.2 18.1 %collective-permute-start.41 = (bf16[256,1408]{1,0:T(8,128)(2,1)S(1)}, bf16[256,1408]{1,0:T(8,128)(2,1)S(1)}, u32[]{:S(2)}, u32[]{:S(2)}) collective-permute-start(bf16[256,1408]{1,0:T(8,128)(2,1)S(1)} %copy-done.117), channel_id=1, source_target_pairs={{0,8},{4,12},{8,0},{12,4},{16,24},{20,28},{24,16},{28,20},{1,9},{5... | collective-permute-start | bytes 2162696 | tf_op jit(solution)/shard_map/ppermute | solution.py:197
  286.3 22.2 %all-to-all-start.4 = ((bf16[4,256,256]{2,1,0:T(8,128)(2,1)}), bf16[4,256,256]{2,1,0:T(8,128)(2,1)S(1)}, u32[]{:S(2)}, u32[]{:S(2)}) async-start(bf16[4,256,256]{2,1,0:T(8,128)(2,1)} %bitcast.37), calls=%async_computation.4 | async-start | bytes 1048576 | tf_op jit(solution)/shard_map/all_to_all | solution.py:233
  308.5 28.7 %all-to-all-start.5 = ((bf16[4,32,2816]{2,1,0:T(8,128)(2,1)}), bf16[4,32,2816]{2,1,0:T(8,128)(2,1)}, u32[]{:S(2)}, u32[]{:S(2)}) async-start(bf16[4,32,2816]{2,1,0:T(8,128)(2,1)} %bitcast.183), calls=%async_computation.5 | async-start | bytes 1441792 | tf_op jit(solution)/shard_map/all_to_all | solution.py:233
  313.2 23.1 %collective-permute-start.44 = (bf16[256,1408]{1,0:T(8,128)(2,1)}, bf16[256,1408]{1,0:T(8,128)(2,1)S(1)}, u32[]{:S(2)}, u32[]{:S(2)}) collective-permute-start(bf16[256,1408]{1,0:T(8,128)(2,1)} %get-tuple-element.380), channel_id=1, source_target_pairs={{0,16},{4,20},{8,24},{12,28},{16,0},{20,4},{24,8},{28,12},{1,17},{... | collective-permute-start | bytes 2162696 | tf_op jit(solution)/shard_map/ppermute | solution.py:197
  314.4 22.7 %collective-permute-start.45 = (bf16[256,1408]{1,0:T(8,128)(2,1)}, bf16[256,1408]{1,0:T(8,128)(2,1)}, u32[]{:S(2)}, u32[]{:S(2)}) collective-permute-start(bf16[256,1408]{1,0:T(8,128)(2,1)} %get-tuple-element.381), channel_id=1, source_target_pairs={{0,8},{4,12},{8,0},{12,4},{16,24},{20,28},{24,16},{28,20},{1,9},{5... | collective-permute-start | bytes 2162696 | tf_op jit(solution)/shard_map/ppermute | solution.py:197
  337.2 20.6 %all-to-all-start.6 = ((bf16[4,256,256]{2,1,0:T(8,128)(2,1)}), bf16[4,256,256]{2,1,0:T(8,128)(2,1)}, u32[]{:S(2)}, u32[]{:S(2)}) async-start(bf16[4,256,256]{2,1,0:T(8,128)(2,1)} %bitcast.176), calls=%async_computation.6 | async-start | bytes 1048576 | tf_op jit(solution)/shard_map/all_to_all | solution.py:233
  357.8 27.8 %all-to-all-start.7 = ((bf16[4,256,256]{2,1,0:T(8,128)(2,1)}), bf16[4,256,256]{2,1,0:T(8,128)(2,1)S(1)}, u32[]{:S(2)}, u32[]{:S(2)}) async-start(bf16[4,256,256]{2,1,0:T(8,128)(2,1)} %bitcast.54), calls=%async_computation.7 | async-start | bytes 1048576 | tf_op jit(solution)/shard_map/all_to_all | solution.py:233
  400.9 25.0 %all-to-all-start.9 = ((bf16[4,32,2816]{2,1,0:T(8,128)(2,1)}), bf16[4,32,2816]{2,1,0:T(8,128)(2,1)}, u32[]{:S(2)}, u32[]{:S(2)}) async-start(bf16[4,32,2816]{2,1,0:T(8,128)(2,1)} %bitcast.182), calls=%async_computation.9 | async-start | bytes 1441792 | tf_op jit(solution)/shard_map/all_to_all | solution.py:233
  425.8 24.7 %collective-permute-start.53 = (bf16[256,2048]{1,0:T(8,128)(2,1)}, bf16[256,2048]{1,0:T(8,128)(2,1)S(1)}, u32[]{:S(2)}, u32[]{:S(2)}) collective-permute-start(bf16[256,2048]{1,0:T(8,128)(2,1)} %get-tuple-element.434), channel_id=1, source_target_pairs={{0,16},{4,20},{8,24},{12,28},{16,0},{20,4},{24,8},{28,12},{1,17},{... | collective-permute-start | bytes 3145736 | tf_op jit(solution)/shard_map/ppermute | solution.py:197
  427.0 24.5 %collective-permute-start.54 = (bf16[256,2048]{1,0:T(8,128)(2,1)}, bf16[256,2048]{1,0:T(8,128)(2,1)}, u32[]{:S(2)}, u32[]{:S(2)}) collective-permute-start(bf16[256,2048]{1,0:T(8,128)(2,1)} %get-tuple-element.435), channel_id=1, source_target_pairs={{0,8},{4,12},{8,0},{12,4},{16,24},{20,28},{24,16},{28,20},{1,9},{5... | collective-permute-start | bytes 3145736 | tf_op jit(solution)/shard_map/ppermute | solution.py:197
  451.5 18.2 %all-to-all-start.11 = ((bf16[4,256,256]{2,1,0:T(8,128)(2,1)}), bf16[4,256,256]{2,1,0:T(8,128)(2,1)S(1)}, u32[]{:S(2)}, u32[]{:S(2)}) async-start(bf16[4,256,256]{2,1,0:T(8,128)(2,1)} %bitcast.67), calls=%async_computation.11 | async-start | bytes 1048576 | tf_op jit(solution)/shard_map/all_to_all | solution.py:233
  469.7 21.7 %all-to-all-start.14 = ((bf16[4,32,2816]{2,1,0:T(8,128)(2,1)}), bf16[4,32,2816]{2,1,0:T(8,128)(2,1)S(1)}, u32[]{:S(2)}, u32[]{:S(2)}) async-start(bf16[4,32,2816]{2,1,0:T(8,128)(2,1)} %bitcast.88), calls=%async_computation.14 | async-start | bytes 1441792 | tf_op jit(solution)/shard_map/all_to_all | solution.py:233
  491.3 36.7 %all-to-all-start.12 = ((bf16[4,32,4096]{2,1,0:T(8,128)(2,1)}), bf16[4,32,4096]{2,1,0:T(8,128)(2,1)}, u32[]{:S(2)}, u32[]{:S(2)}) async-start(bf16[4,32,4096]{2,1,0:T(8,128)(2,1)} %bitcast.76), calls=%async_computation.12 | async-start | bytes 2097152 | tf_op jit(solution)/shard_map/all_to_all | solution.py:233
  536.8 18.7 %all-to-all-start.13 = ((bf16[4,32,2048]{2,1,0:T(8,128)(2,1)}), bf16[4,32,2048]{2,1,0:T(8,128)(2,1)S(1)}, u32[]{:S(2)}, u32[]{:S(2)}) async-start(bf16[4,32,2048]{2,1,0:T(8,128)(2,1)} %bitcast.184), calls=%async_computation.13 | async-start | bytes 1048576 | tf_op jit(solution)/shard_map/all_to_all | solution.py:233
  (173 other events, 1684.4 us)
